TPU v7x, 32 devices: a whole 2x2x4 slice. The times are simulated.
32 devices in a mesh: seq: 8 (over z, x), head: 4 (over y, core).
Axes of the slice: x: 2, y: 2, z: 4, core: 2. Of those that a mesh axis runs over, the one named last changes fastest.
Arguments:
- image_input_rows: bfloat16 [1024, 3072], P(('seq', 'head')), may hold values from -6 to 6
- adapter_down_weight: bfloat16 [3072, 64], replicated, may hold values from -0.109375 to 0.109375
- adapter_up_weight: bfloat16 [64, 1536], replicated, may hold values from -0.75 to 0.75
- image_query_rows: bfloat16 [1024, 1536], P(('seq', 'head')), may hold values from -72 to 72
- image_key_rows: bfloat16 [1024, 1536], P(('seq', 'head')), may hold values from -4 to 4
- image_value_codes: int32 [1024, 1536], P(('seq', 'head')), may hold values from -127 to 127
- value_fraction: bfloat16 [1024, 1536], P(('seq', 'head')), may hold values from -0.5 to 0.5
- value_step_sizes: float32 [8, 12], replicated, may hold values from 0.004 to 0.03
- timestep_group: int32 [1000], replicated, may hold values from 0 to 7
- timestep: int32 [1], replicated, may hold values from 0 to 999
- image_output_grad: bfloat16 [1024, 1536], P(('seq', 'head')), may hold values from -1960 to 1960
- text_query_rows: bfloat16 [512, 1536], P(None, 'head'), may hold values from -4 to 4
- text_key_rows: bfloat16 [512, 1536], P(None, 'head'), may hold values from -4 to 4
- text_value_rows: bfloat16 [512, 1536], P(None, 'head'), may hold values from -4 to 4
- text_output_grad: bfloat16 [512, 1536], P(None, 'head'), may hold values from -512 to 512
Outputs:
- dq_img: bfloat16 [1024, 1536], P(('seq', 'head'))
- dk_img: bfloat16 [1024, 1536], P(('seq', 'head'))
- image_value_grad: bfloat16 [1024, 1536], P(('seq', 'head'))
- dq_txt: bfloat16 [512, 1536], P('seq', 'head')
- dk_txt: bfloat16 [512, 1536], P('seq', 'head')
- dv_txt: bfloat16 [512, 1536], P('seq', 'head')
- grad_down: float32 [3072, 64], replicated
- grad_up: float32 [64, 1536], replicated
- grad_steps: float32 [8, 12], replicated
All inputs are finite; a program needn't handle non-finite values.
Results may differ from a plain program's by a relative error of at most 0.013.
Values may be sent and summed in bfloat16 or wider, within the bound.
A program may use at most 128 MiB of HBM per device.

v0:
```python
import math

import jax
import jax.numpy as jnp
from jax import lax
from jax.sharding import PartitionSpec as P

HEAD_SIZE = 128
QMAX = 127


unscale = 0.0078125


def split_heads(rows):
    return rows.reshape(rows.shape[0], rows.shape[1] // HEAD_SIZE, HEAD_SIZE)


def join_heads(heads):
    return heads.reshape(heads.shape[0], heads.shape[1] * heads.shape[2])


def head_scores(queries, key_rows):
    return jnp.einsum(
        "qhd,khd->hqk", queries, key_rows, preferred_element_type=jnp.float32
    ) * HEAD_SIZE ** (-0.5)


def over_keys(step_fn, initial, key_rows, value_rows):
    block_rows = math.gcd(key_rows.shape[0], 2048)

    def over_one_turn(turn_index, carried):
        key_block = lax.dynamic_slice_in_dim(key_rows, turn_index * block_rows, block_rows, 0)
        value_block = lax.dynamic_slice_in_dim(value_rows, turn_index * block_rows, block_rows, 0)
        return step_fn(carried, key_block, value_block)

    return lax.fori_loop(0, key_rows.shape[0] // block_rows, over_one_turn, initial)


def key_terms(carried, queries, grads, log_rows, delta_rows, own_keys, own_values):
    key_grad, value_grad = carried
    probs = jnp.exp(head_scores(queries, own_keys) - log_rows.T[:, :, None])
    dprobs = jnp.einsum("qhd,khd->hqk", grads, own_values, preferred_element_type=jnp.float32)
    dscores = (probs * (dprobs - delta_rows.T[:, :, None])).astype(jnp.bfloat16)
    value_grad = value_grad + jnp.einsum(
        "hqk,qhd->khd", probs.astype(jnp.bfloat16), grads, preferred_element_type=jnp.float32
    )
    key_grad = key_grad + jnp.einsum(
        "hqk,qhd->khd", dscores, queries, preferred_element_type=jnp.float32
    ) * HEAD_SIZE ** (-0.5)
    return (key_grad, value_grad)


def on_device(
    image_input_rows,
    adapter_down_weight,
    adapter_up_weight,
    image_query_rows,
    image_key_rows,
    image_value_codes,
    value_fraction,
    value_step_sizes,
    timestep_group,
    timestep,
    image_output_grad,
    text_query_rows,
    text_key_rows,
    text_value_rows,
    text_output_grad,
):
    slot_index = jnp.sum(
        jnp.where(
            jnp.arange(timestep_group.shape[0], dtype=jnp.int32) == timestep[0], timestep_group, 0
        )
    )
    slot_rows = jnp.arange(value_step_sizes.shape[0], dtype=jnp.int32) == slot_index
    step_row = jnp.sum(jnp.where(slot_rows[:, None], value_step_sizes, 0.0), axis=0)
    code_values = image_value_codes.astype(jnp.float32)
    v_dequant = (code_values * jnp.repeat(step_row, HEAD_SIZE)[None, :]).astype(jnp.bfloat16)
    inside = jnp.abs(image_value_codes) < QMAX
    lsq_term = jnp.where(inside, -value_fraction.astype(jnp.float32), code_values)
    query_img, key_img, value_img, grad_img = (
        lax.all_to_all(image_query_rows, "head", split_axis=1, concat_axis=0, tiled=True),
        lax.all_to_all(image_key_rows, "head", split_axis=1, concat_axis=0, tiled=True),
        lax.all_to_all(v_dequant, "head", split_axis=1, concat_axis=0, tiled=True),
        lax.all_to_all(image_output_grad, "head", split_axis=1, concat_axis=0, tiled=True),
    )
    share_rows = text_query_rows.shape[0] // lax.axis_size("seq")
    first_row = lax.axis_index("seq") * share_rows

    def own_rows(table):
        return lax.dynamic_slice_in_dim(table, first_row, share_rows, 0)

    image_rows = query_img.shape[0]
    query_local = jnp.concatenate([query_img, own_rows(text_query_rows)], axis=0)
    grad_local = jnp.concatenate([grad_img, own_rows(text_output_grad)], axis=0)
    query_split = split_heads(query_local)
    grad_split = split_heads(grad_local)
    local_count = query_split.shape[0]
    head_count = query_split.shape[1]
    key_image, value_image = (
        lax.all_gather(key_img, "seq", axis=0, tiled=True),
        lax.all_gather(value_img, "seq", axis=0, tiled=True),
    )
    text_keys = split_heads(text_key_rows)
    text_values = split_heads(text_value_rows)
    key_sets = ((split_heads(key_image), split_heads(value_image)), (text_keys, text_values))

    def stat_turn(carried, key_block, value_block):
        row_max, running, weighted = carried
        scores = head_scores(query_split, key_block)
        dprobs = jnp.einsum(
            "qhd,khd->hqk", grad_split, value_block, preferred_element_type=jnp.float32
        )
        new_max = jnp.maximum(row_max, jnp.max(scores, axis=2, keepdims=True))
        factor = jnp.exp(row_max - new_max)
        expo = jnp.exp(scores - new_max)
        running = running * factor + jnp.sum(expo, axis=2, keepdims=True)
        weighted = weighted * factor + jnp.sum(expo * dprobs, axis=2, keepdims=True)
        return (new_max, running, weighted)

    row_stats = (
        jnp.full((head_count, local_count, 1), -jnp.inf, jnp.float32),
        jnp.zeros((head_count, local_count, 1), jnp.float32),
        jnp.zeros((head_count, local_count, 1), jnp.float32),
    )
    for key_rows, value_rows in key_sets:
        row_stats = over_keys(stat_turn, row_stats, key_rows, value_rows)
    log_sums = row_stats[0] + jnp.log(row_stats[1])
    deltas = row_stats[2] / row_stats[1]

    def query_turn(running, key_block, value_block):
        probs = jnp.exp(head_scores(query_split, key_block) - log_sums)
        dprobs = jnp.einsum(
            "qhd,khd->hqk", grad_split, value_block, preferred_element_type=jnp.float32
        )
        dscores = (probs * (dprobs - deltas)).astype(jnp.bfloat16)
        return running + jnp.einsum(
            "hqk,khd->qhd", dscores, key_block, preferred_element_type=jnp.float32
        ) * HEAD_SIZE ** (-0.5)

    query_grad = jnp.zeros((local_count, head_count, HEAD_SIZE), jnp.float32)
    for key_rows, value_rows in key_sets:
        query_grad = over_keys(query_turn, query_grad, key_rows, value_rows)
    query_grad = join_heads(query_grad).astype(jnp.bfloat16)
    log_rows = log_sums[:, :, 0].T
    delta_rows = deltas[:, :, 0].T
    own_keys = split_heads(key_img)
    own_values = split_heads(value_img)
    empty = jnp.zeros(own_keys.shape, jnp.float32)
    query_rows = lax.all_gather(query_local.astype(jnp.float32), "seq", axis=0, tiled=True).astype(
        jnp.bfloat16
    )
    grad_rows = lax.all_gather(grad_local.astype(jnp.float32), "seq", axis=0, tiled=True).astype(
        jnp.bfloat16
    )
    log_part = lax.all_gather(log_rows, "seq", axis=0, tiled=True)
    delta_part = lax.all_gather(delta_rows, "seq", axis=0, tiled=True)
    piece_rows = query_rows.shape[0]
    block_rows = piece_rows if piece_rows <= 2048 else math.gcd(piece_rows, 2048)

    def fold_one_turn(turn_index, running):

        def rows_of(table):
            return lax.dynamic_slice_in_dim(table, turn_index * block_rows, block_rows, 0)

        return key_terms(
            running,
            split_heads(rows_of(query_rows)),
            split_heads(rows_of(grad_rows)),
            rows_of(log_part),
            rows_of(delta_part),
            own_keys,
            own_values,
        )

    key_grad, value_grad = lax.fori_loop(0, piece_rows // block_rows, fold_one_turn, (empty, empty))
    key_grad = join_heads(key_grad).astype(jnp.bfloat16)
    value_grad = join_heads(value_grad).astype(jnp.bfloat16)
    text_empty = jnp.zeros(text_keys.shape, jnp.float32)
    text_key, text_value = key_terms(
        (text_empty, text_empty),
        query_split,
        grad_split,
        log_rows,
        delta_rows,
        text_keys,
        text_values,
    )
    text_key, text_value = (
        lax.psum_scatter(join_heads(text_key), "seq", scatter_dimension=0, tiled=True),
        lax.psum_scatter(join_heads(text_value), "seq", scatter_dimension=0, tiled=True),
    )
    dk_txt = text_key.astype(jnp.bfloat16)
    dv_txt = text_value.astype(jnp.bfloat16)
    dq_txt = query_grad[image_rows:]
    dq_heads = query_grad[:image_rows]
    dq_img, dk_img, dv_quant = (
        lax.all_to_all(dq_heads, "head", split_axis=0, concat_axis=1, tiled=True),
        lax.all_to_all(key_grad, "head", split_axis=0, concat_axis=1, tiled=True),
        lax.all_to_all(value_grad, "head", split_axis=0, concat_axis=1, tiled=True),
    )
    image_value_grad = jnp.where(inside, dv_quant, jnp.zeros_like(dv_quant))
    lowrank_gradient = jnp.einsum(
        "vg,zg->vz", image_value_grad, adapter_up_weight, preferred_element_type=jnp.float32
    ).astype(jnp.bfloat16)
    part_down = jnp.einsum(
        "td,tr->dr", image_input_rows, lowrank_gradient, preferred_element_type=jnp.float32
    )
    lowrank_input = jnp.dot(
        image_input_rows, adapter_down_weight, preferred_element_type=jnp.float32
    ).astype(jnp.bfloat16)
    part_up = jnp.einsum(
        "tr,tw->rw", lowrank_input, image_value_grad, preferred_element_type=jnp.float32
    )
    token_rows = dv_quant.shape[0]
    token_terms = (dv_quant.astype(jnp.float32) * lsq_term).reshape(
        token_rows, value_step_sizes.shape[1], HEAD_SIZE
    )
    total_down, total_up, step_sums = lax.psum(
        (part_down, part_up, jnp.sum(token_terms, axis=(0, 2))), ("seq", "head")
    )
    grad_steps = jnp.where(slot_rows[:, None], step_sums[None, :], 0.0) * (QMAX ** (-0.5) * unscale)
    return (
        dq_img,
        dk_img,
        image_value_grad,
        dq_txt,
        dk_txt,
        dv_txt,
        total_down * unscale,
        total_up * unscale,
        grad_steps,
    )


def solution(mesh):
    placed = (
        P(("seq", "head"), None),
        P(),
        P(),
        P(("seq", "head"), None),
        P(("seq", "head"), None),
        P(("seq", "head"), None),
        P(("seq", "head"), None),
        P(),
        P(),
        P(),
        P(("seq", "head"), None),
        P(None, "head"),
        P(None, "head"),
        P(None, "head"),
        P(None, "head"),
    )
    return jax.shard_map(
        on_device,
        mesh=mesh,
        in_specs=placed,
        out_specs=(
            P(("seq", "head"), None),
            P(("seq", "head"), None),
            P(("seq", "head"), None),
            P("seq", "head"),
            P("seq", "head"),
            P("seq", "head"),
            P(),
            P(),
            P(),
        ),
        check_vma=False,
    )
```

profile of v0, /device:TPU:0, one launch (start us, length us, event | category | flops | bytes accessed | tf_op | source)
XLA Modules:
  0.0 423.0 jit_solution(4455836994622354287)
XLA Ops:
  8.9 4.2 %all-to-all-start = ((bf16[32,4,384]{2,0,1:T(8,128)(2,1)}), bf16[32,4,384]{2,0,1:T(8,128)(2,1)S(1)}, u32[]{:S(2)}, u32[]{:S(2)}) async-start(bf16[32,4,384]{2,0,1:T(8,128)(2,1)} %bitcast.176), calls=%async_computation | async-start | bytes 196608 | tf_op jit(solution)/shard_map/all_to_all | solution.py:83
  17.4 3.4 all-to-all-start.1
  26.5 3.3 all-to-all-start.2
  29.8 34.3 %all_gather.18 = bf16[1024,384]{1,0:T(8,128)(2,1)S(1)} all-gather(bf16[128,384]{1,0:T(8,128)(2,1)S(1)} %bitcast.192), channel_id=1, replica_groups=mesh['seq'=8,'head'=4] {'seq'}, dimensions={0}, use_global_device_ids=true | all-gather | bytes 884736 | tf_op jit(solution)/shard_map/all_gather | solution.py:102
  64.4 3.3 all-to-all-start.3
  72.0 34.1 %all_gather.19 = bf16[1024,384]{1,0:T(8,128)(2,1)} all-gather(bf16[128,384]{1,0:T(8,128)(2,1)S(1)} %bitcast.190), channel_id=1, replica_groups=mesh['seq'=8,'head'=4] {'seq'}, dimensions={0}, use_global_device_ids=true | all-gather | bytes 884736 | tf_op jit(solution)/shard_map/all_gather | solution.py:103
  109.2 2.3 copy.181
  115.2 2.3 fusion.4
  121.4 2.3 copy.202
  125.2 2.5 fusion.15
  129.2 3.3 all-to-all-start.4
  133.3 30.4 %all-gather = f32[8,192,3]{1,2,0:T(4,128)S(1)} all-gather(f32[1,192,3]{1,2,0:T(4,128)S(1)} %get-tuple-element.116), channel_id=1, replica_groups=mesh['seq'=8,'head'=4] {'seq'}, dimensions={0}, use_global_device_ids=true | all-gather | bytes 20736 | tf_op jit(solution)/shard_map/all_gather | solution.py:157
  167.3 2.4 copy.189
  171.9 2.4 copy.193
  174.3 2.4 fusion.19
  178.6 3.9 all-to-all-start.6
  184.0 30.4 %all-gather.1 = f32[8,192,3]{1,2,0:T(4,128)S(1)} all-gather(f32[1,192,3]{1,2,0:T(4,128)S(1)} %get-tuple-element.115), channel_id=1, replica_groups=mesh['seq'=8,'head'=4] {'seq'}, dimensions={0}, use_global_device_ids=true | all-gather | bytes 20736 | tf_op jit(solution)/shard_map/all_gather | solution.py:158
  217.7 2.3 fusion.23
  220.0 2.4 convolution_bitcast_fusion
  222.4 2.9 fusion.22
  226.2 3.4 all-to-all-start.5
  229.8 47.4 %reduce-scatter.5.cloned.1.call-done = f32[64,384]{1,0:T(8,128)} async-done(((f32[512,384]{1,0:T(8,128)}), f32[64,384]{1,0:T(8,128)}) %reduce-scatter.5.cloned.1.call-update) | async-done | bytes 98320 | tf_op jit(solution)/shard_map/reduce_scatter | solution.py:192
  278.7 40.2 %psum.23 = f32[12]{0:T(128)S(1)} all-reduce(f32[12]{0:T(128)S(1)} %bitcast_reduce_fusion), channel_id=1, replica_groups=mesh['seq'=8,'head'=4] {'seq','head'}, use_global_device_ids=true, to_apply=%region_14.15 | all-reduce | flops 12 | bytes 96 | tf_op jit(solution)/shard_map/psum | solution.py:220
  320.2 93.4 %all-reduce.3.cloned.1.call-done = (f32[3072,64]{0,1:T(8,128)}, f32[64,1536]{1,0:T(8,128)}) async-done(((f32[3072,64]{0,1:T(8,128)}, f32[64,1536]{1,0:T(8,128)}), (f32[3072,64]{0,1:T(8,128)}, f32[64,1536]{1,0:T(8,128)})) %all-reduce.3.cloned.1.call-update) | async-done | bytes 1179664 | tf_op jit(solution)/shard_map/psum | solution.py:220
  (139 shorter events, 48.9 us)
Async XLA Ops:
  7.2 8.1 %copy-start = (bf16[512,384]{1,0:T(8,128)(2,1)S(1)}, bf16[512,384]{1,0:T(8,128)(2,1)}, u32[]{:S(2)}) copy-start(bf16[512,384]{1,0:T(8,128)(2,1)} %param.26) | copy-start | bytes 1179652
  7.2 15.1 %copy-start.17 = (bf16[512,384]{1,0:T(8,128)(2,1)S(1)}, bf16[512,384]{1,0:T(8,128)(2,1)}, u32[]{:S(2)}) copy-start(bf16[512,384]{1,0:T(8,128)(2,1)} %param.27) | copy-start | bytes 1179652
  7.2 16.0 %copy-start.20 = (bf16[32,1536]{1,0:T(8,128)(2,1)S(1)}, bf16[32,1536]{1,0:T(8,128)(2,1)}, u32[]{:S(2)}) copy-start(bf16[32,1536]{1,0:T(8,128)(2,1)} %param.25) | copy-start | bytes 294916
  7.2 16.6 %copy-start.18 = (bf16[512,384]{1,0:T(8,128)(2,1)S(1)}, bf16[512,384]{1,0:T(8,128)(2,1)}, u32[]{:S(2)}) copy-start(bf16[512,384]{1,0:T(8,128)(2,1)} %param.28) | copy-start | bytes 1179652
  8.9 8.5 %all-to-all-start = ((bf16[32,4,384]{2,0,1:T(8,128)(2,1)}), bf16[32,4,384]{2,0,1:T(8,128)(2,1)S(1)}, u32[]{:S(2)}, u32[]{:S(2)}) async-start(bf16[32,4,384]{2,0,1:T(8,128)(2,1)} %bitcast.176), calls=%async_computation | async-start | bytes 196608 | tf_op jit(solution)/shard_map/all_to_all | solution.py:83
  17.4 9.1 %all-to-all-start.1 = ((bf16[32,4,384]{2,0,1:T(8,128)(2,1)}), bf16[32,4,384]{2,0,1:T(8,128)(2,1)S(1)}, u32[]{:S(2)}, u32[]{:S(2)}) async-start(bf16[32,4,384]{2,0,1:T(8,128)(2,1)} %bitcast.175), calls=%async_computation.1 | async-start | bytes 196608 | tf_op jit(solution)/shard_map/all_to_all | solution.py:84
  20.8 146.5 %all-gather.5.cloned.1.call-start = ((), (), s32[]{:S(2)}) async-start(), calls=%async_computation.9 | async-start | bytes 1327104 | tf_op jit(solution)/shard_map/all_gather | solution.py:151
  26.5 37.6 %copy-start.11 = (bf16[32,4,384]{2,0,1:T(8,128)(2,1)}, bf16[32,4,384]{2,0,1:T(8,128)(2,1)S(1)}, u32[]{:S(2)}) copy-start(bf16[32,4,384]{2,0,1:T(8,128)(2,1)S(1)} %all-to-all-done.1) | copy-start | bytes 294916
  26.5 37.9 %all-to-all-start.2 = ((bf16[32,4,384]{2,0,1:T(8,128)(2,1)}), bf16[32,4,384]{2,0,1:T(8,128)(2,1)S(1)}, u32[]{:S(2)}, u32[]{:S(2)}) async-start(bf16[32,4,384]{2,0,1:T(8,128)(2,1)} %bitcast.174), calls=%async_computation.2 | async-start | bytes 196608 | tf_op jit(solution)/shard_map/all_to_all | solution.py:86
  64.4 41.7 %copy-start.13 = (bf16[32,4,384]{2,0,1:T(8,128)(2,1)}, bf16[32,4,384]{2,0,1:T(8,128)(2,1)S(1)}, u32[]{:S(2)}) copy-start(bf16[32,4,384]{2,0,1:T(8,128)(2,1)S(1)} %all-to-all-done.2) | copy-start | bytes 294916
  64.4 7.6 %all-to-all-start.3 = ((bf16[32,4,384]{2,0,1:T(8,128)(2,1)}), bf16[32,4,384]{2,0,1:T(8,128)(2,1)S(1)}, u32[]{:S(2)}, u32[]{:S(2)}) async-start(bf16[32,4,384]{2,0,1:T(8,128)(2,1)} %bitcast.173), calls=%async_computation.3 | async-start | bytes 196608 | tf_op jit(solution)/shard_map/all_to_all | solution.py:85
  67.8 104.2 %all-gather.7.cloned.1.call-start = ((), (), s32[]{:S(2)}) async-start(), calls=%async_computation.10 | async-start | bytes 1327104 | tf_op jit(solution)/shard_map/all_gather | solution.py:154
  72.0 34.1 %copy-start.9 = (bf16[32,4,384]{2,0,1:T(8,128)(2,1)}, bf16[32,4,384]{2,0,1:T(8,128)(2,1)S(1)}, u32[]{:S(2)}) copy-start(bf16[32,4,384]{2,0,1:T(8,128)(2,1)S(1)} %all-to-all-done.3) | copy-start | bytes 294916
  106.1 109.1 %reduce-scatter.3.cloned.1.call-start = ((), (), s32[]{:S(2)}) async-start(), calls=%async_computation.11 | async-start | bytes 884736 | tf_op jit(solution)/shard_map/reduce_scatter | solution.py:191
  128.3 36.4 %copy-start.2 = (f32[3,192,512]{2,1,0:T(8,128)S(1)}, f32[3,192,512]{2,1,0:T(8,128)}, u32[]{:S(2)}) copy-start(f32[3,192,512]{2,1,0:T(8,128)} %copy-done.1) | copy-start | bytes 3538948
  129.2 49.4 %all-to-all-start.4 = ((bf16[4,32,384]{2,1,0:T(8,128)(2,1)}), bf16[4,32,384]{2,1,0:T(8,128)(2,1)S(1)}, u32[]{:S(2)}, u32[]{:S(2)}) async-start(bf16[4,32,384]{2,1,0:T(8,128)(2,1)} %all_to_all.108), calls=%async_computation.4 | async-start | bytes 196608 | tf_op jit(solution)/shard_map/all_to_all | solution.py:199
  132.5 144.7 %reduce-scatter.5.cloned.1.call-start = ((), (), s32[]{:S(2)}) async-start(), calls=%async_computation.12 | async-start | bytes 884736 | tf_op jit(solution)/shard_map/reduce_scatter | solution.py:192
  174.3 40.1 %copy-start.10 = (bf16[32,4,384]{2,0,1:T(8,128)(2,1)S(1)}, bf16[32,4,384]{2,0,1:T(8,128)(2,1)}, u32[]{:S(2)}) copy-start(bf16[32,4,384]{2,0,1:T(8,128)(2,1)} %copy-done.9) | copy-start | bytes 294916
  176.8 40.9 %copy-start.7 = (s32[32,1536]{1,0:T(8,128)S(1)}, s32[32,1536]{1,0:T(8,128)}, u32[]{:S(2)}) copy-start(s32[32,1536]{1,0:T(8,128)} %param.20) | copy-start | bytes 589828
  176.8 40.9 %copy-start.14 = (bf16[32,3072]{1,0:T(8,128)(2,1)S(1)}, bf16[32,3072]{1,0:T(8,128)(2,1)}, u32[]{:S(2)}) copy-start(bf16[32,3072]{1,0:T(8,128)(2,1)} %param.15) | copy-start | bytes 589828
  178.6 38.1 %all-to-all-start.6 = ((bf16[4,32,384]{2,1,0:T(8,128)(2,1)}), bf16[4,32,384]{2,1,0:T(8,128)(2,1)}, u32[]{:S(2)}, u32[]{:S(2)}) async-start(bf16[4,32,384]{2,1,0:T(8,128)(2,1)} %convert_element_type.100), calls=%async_computation.6 | async-start | bytes 196608 | tf_op jit(solution)/shard_map/all_to_all | solution.py:201
  182.5 231.0 %all-reduce.3.cloned.1.call-start = ((), (), s32[]{:S(2)}) async-start(), calls=%async_computation.13 | async-start | bytes 2359296 | tf_op jit(solution)/shard_map/psum | solution.py:220
  225.3 94.2 %copy-start.29 = (pred[8]{0:T(512)(128)(4,1)S(1)}, pred[8]{0:T(512)(128)(4,1)}, u32[]{:S(2)}) copy-start(pred[8]{0:T(512)(128)(4,1)} %copy-done.28) | copy-start | bytes 28
  226.2 92.7 %all-to-all-start.5 = ((bf16[4,32,384]{2,1,0:T(8,128)(2,1)}), bf16[4,32,384]{2,1,0:T(8,128)(2,1)S(1)}, u32[]{:S(2)}, u32[]{:S(2)}) async-start(bf16[4,32,384]{2,1,0:T(8,128)(2,1)} %convert_element_type.96), calls=%async_computation.5 | async-start | bytes 196608 | tf_op jit(solution)/shard_map/all_to_all | solution.py:200
  (18 other events, 52.2 us)
Sparse Core Ops, SparseCore 0:
  23.9 47.6 all-gather.4
  106.2 40.7 all-gather.6
  150.4 61.2 reduce-scatter.2
  215.7 61.3 reduce-scatter.4
  283.1 130.4 all-reduce.2
where the time goes:
time: 425 us; the launch traced here: 423 us
  blocking collectives  169 us (40%)
  waiting for transfers between devices  144 us (34%)
  local copies, waits for them, and re-layouts  32.9 us (8%)
  matrix products  25.5 us (6%)
  starting transfers between devices  25.1 us (6%)
  between operations  14.9 us (4%)
  other arithmetic  11.3 us (3%)
    psum x1, waiting for transfers between devices, on_device(): lax.psum((part_down, part_up, jnp.sum(token_terms, axis=(0, 2))), ('seq',...  93.4 us
    reduce_scatter x1, waiting for transfers between devices, on_device(): lax.psum_scatter(join_heads(text_value), 'seq', scatter_dimension=0, tile...  47.4 us
    psum x1, blocking collectives, on_device(): lax.psum((part_down, part_up, jnp.sum(token_terms, axis=(0, 2))), ('seq',...  40.2 us
    all_gather x1, blocking collectives, on_device(): lax.all_gather(key_img, 'seq', axis=0, tiled=True)  34.3 us
    all_gather x1, blocking collectives, on_device(): lax.all_gather(value_img, 'seq', axis=0, tiled=True)  34.1 us
    all_gather x1, blocking collectives, on_device(): log_part = lax.all_gather(log_rows, 'seq', axis=0, tiled=True)  30.4 us
    all_gather x1, blocking collectives, on_device(): delta_part = lax.all_gather(delta_rows, 'seq', axis=0, tiled=True)  30.4 us
  transfers between devices with their start and end apart: 12, of which 4 were waited for; matrix products, arithmetic and copies ran while one was open for 15% of the time, Pallas kernels for 0%

commit v1 on v0

--- a/solution.py
+++ b/solution.py
@@ -1,8 +1,11 @@
+import functools
 import math
 
 import jax
 import jax.numpy as jnp
 from jax import lax
+from jax.experimental import pallas as pl
+from jax.experimental.pallas import tpu as pltpu
 from jax.sharding import PartitionSpec as P
 
 HEAD_SIZE = 128
@@ -234,6 +237,462 @@
     )
 
 
+MESH = pl.DeviceIdType.MESH
+BF = jnp.bfloat16
+F32 = jnp.float32
+NT = (((1,), (1,)), ((), ()))
+NN = (((1,), (0,)), ((), ()))
+
+
+def dot(left, right, dims=NN):
+    return lax.dot_general(left, right, dims, preferred_element_type=F32)
+
+
+def attention_kernel(
+    seq,
+    head,
+    q_ref,
+    k_ref,
+    code_ref,
+    do_ref,
+    tq_ref,
+    tk_ref,
+    tv_ref,
+    tdo_ref,
+    step_ref,
+    dq_ref,
+    dk_ref,
+    dv_ref,
+    dqt_ref,
+    dkt_ref,
+    dvt_ref,
+    stage,
+    recv,
+    kv2,
+    tkv,
+    tqd,
+    kall,
+    ktr,
+    vall,
+    qall,
+    doall,
+    dqall,
+    dkacc,
+    dvacc,
+    xo,
+    xi,
+    to,
+    ti,
+    ost,
+    ret,
+    tfin,
+    rett,
+    s1,
+    r1,
+    s2,
+    r2,
+    st,
+    rt,
+    s3,
+    r3,
+    s4,
+    r4,
+    s5,
+    r5,
+):
+    rows = q_ref.shape[0]
+    heads = q_ref.shape[1] // HEAD_SIZE
+    text = tq_ref.shape[0]
+    half = text // 2
+    planes = head // 2
+    peers = seq * planes
+    group = tq_ref.shape[1] // HEAD_SIZE
+    pair = 2 * group
+    first = (seq - pair) // 2
+    image = peers * rows
+    share = text // seq
+    scale = HEAD_SIZE ** (-0.5)
+
+    s = lax.axis_index("seq")
+    g = lax.axis_index("head")
+    c = lax.rem(g, 2)
+    y = g // 2
+    me = s * planes + y
+    partner = (s, g + 1 - 2 * c)
+    slot = s - first
+    is_head = jnp.logical_and(slot >= 0, slot < pair)
+    mine = y * pair + slot
+    holds_text = jnp.logical_and(is_head, slot // group == c)
+    takes_text = jnp.logical_and(is_head, slot // group != c)
+    lane_block = lax.rem(slot, group)
+
+    def peer(p):
+        return (p // planes, (p % planes) * 2 + c)
+
+    def home(h):
+        return (first + h % pair, (h // pair) * 2 + c)
+
+    def home_peer(h):
+        return (first + h % pair) * planes + h // pair
+
+    def send(src, dst, ssem, rsem, to_id):
+        return pltpu.make_async_remote_copy(
+            src_ref=src, dst_ref=dst, send_sem=ssem, recv_sem=rsem, device_id=to_id, device_id_type=MESH
+        )
+
+    barrier = pltpu.get_barrier_semaphore()
+    for p in range(peers):
+
+        @pl.when(me != p)
+        def _():
+            pl.semaphore_signal(barrier, inc=1, device_id=peer(p), device_id_type=MESH)
+
+    pl.semaphore_signal(barrier, inc=1, device_id=partner, device_id_type=MESH)
+
+    for h in range(heads):
+        cols = slice(h * HEAD_SIZE, (h + 1) * HEAD_SIZE)
+        stage[h, 0:rows] = k_ref[:, cols]
+        stage[h, rows : 2 * rows] = code_ref[:, cols].astype(F32).astype(BF)
+        stage[h, 2 * rows : 3 * rows] = q_ref[:, cols]
+        stage[h, 3 * rows : 4 * rows] = do_ref[:, cols]
+
+    pl.semaphore_wait(barrier, peers)
+
+    def first_send(h):
+        return send(stage.at[h], recv.at[me], s1.at[h], r1.at[me], home(h))
+
+    def first_recv(p):
+        return send(stage.at[0], recv.at[p], s1.at[0], r1.at[p], partner)
+
+    for h in range(heads):
+
+        @pl.when(me != home_peer(h))
+        def _():
+            first_send(h).start()
+
+    def text_copies():
+        cols = pl.ds(pl.multiple_of(lane_block * HEAD_SIZE, HEAD_SIZE), HEAD_SIZE)
+        low = pl.ds(half, half)
+        return (
+            send(tk_ref.at[:, cols], tkv.at[0], st.at[0], rt.at[0], partner),
+            send(tv_ref.at[:, cols], tkv.at[1], st.at[1], rt.at[1], partner),
+            send(tq_ref.at[low, cols], tqd.at[0], st.at[2], rt.at[2], partner),
+            send(tdo_ref.at[low, cols], tqd.at[1], st.at[3], rt.at[3], partner),
+        )
+
+    @pl.when(holds_text)
+    def _():
+        for copy in text_copies():
+            copy.start()
+        cols = pl.ds(pl.multiple_of(lane_block * HEAD_SIZE, HEAD_SIZE), HEAD_SIZE)
+        kall[2 * image : 2 * image + text] = tk_ref[:, cols]
+        vall[2 * image : 2 * image + text] = tv_ref[:, cols]
+        qall[image : image + half] = tq_ref[0:half, cols]
+        doall[image : image + half] = tdo_ref[0:half, cols]
+
+    @pl.when(is_head)
+    def _():
+        recv[pl.ds(me, 1)] = stage[pl.ds(mine, 1)]
+        for p in range(peers):
+
+            @pl.when(me != p)
+            def _():
+                first_recv(p).wait_recv()
+
+        swap = send(recv.at[:, pl.ds(0, 2 * rows)], kv2, s2.at[0], r2.at[0], partner)
+        swap.start()
+        step = step_ref[:, pl.ds(pl.multiple_of(mine * HEAD_SIZE, HEAD_SIZE), HEAD_SIZE)]
+
+        def dequant(codes):
+            return (codes.reshape(image, HEAD_SIZE).astype(F32) * step).astype(BF)
+
+        kall[0:image] = recv[:, 0:rows].reshape(image, HEAD_SIZE)
+        vall[0:image] = dequant(recv[:, rows : 2 * rows])
+        qall[0:image] = recv[:, 2 * rows : 3 * rows].reshape(image, HEAD_SIZE)
+        doall[0:image] = recv[:, 3 * rows : 4 * rows].reshape(image, HEAD_SIZE)
+
+        @pl.when(takes_text)
+        def _():
+            for copy in text_copies():
+                copy.wait_recv()
+            kall[2 * image : 2 * image + text] = tkv[0]
+            vall[2 * image : 2 * image + text] = tkv[1]
+            qall[image : image + half] = tqd[0]
+            doall[image : image + half] = tqd[1]
+
+        swap.wait_recv()
+        kall[image : 2 * image] = kv2[:, 0:rows].reshape(image, HEAD_SIZE)
+        vall[image : 2 * image] = dequant(kv2[:, rows : 2 * rows])
+        ktr[...] = kall[...].T
+        dkacc[...] = jnp.zeros_like(dkacc)
+        dvacc[...] = jnp.zeros_like(dvacc)
+
+        def query_block(index, carried):
+            at = pl.ds(pl.multiple_of(index * half, half), half)
+            queries, grads = qall[at], doall[at]
+            scores = dot(kall[...], queries, NT) * scale
+            expo = jnp.exp(scores - jnp.max(scores, axis=0, keepdims=True))
+            probs = expo * (1.0 / jnp.sum(expo, axis=0, keepdims=True))
+            dvacc[...] += dot(probs.astype(BF), grads)
+            dprobs = dot(vall[...], grads, NT)
+            deltas = jnp.sum(probs * dprobs, axis=0, keepdims=True)
+            dscores = (probs * (dprobs - deltas)).astype(BF)
+            dkacc[...] += dot(dscores, queries)
+            dqall[at] = (dot(ktr[...], dscores).T * scale).astype(BF)
+            return carried
+
+        lax.fori_loop(0, (image + half) // half, query_block, 0)
+        xo[0] = (dkacc[image : 2 * image] * scale).astype(BF)
+        xo[1] = dvacc[image : 2 * image].astype(BF)
+        trade = send(xo, xi, s3.at[0], r3.at[0], partner)
+        trade.start()
+        text_trade = send(to, ti, s3.at[1], r3.at[1], partner)
+
+        @pl.when(takes_text)
+        def _():
+            to[0:text] = (dkacc[2 * image : 2 * image + text] * scale).astype(BF)
+            to[text : 2 * text] = dvacc[2 * image : 2 * image + text].astype(BF)
+            to[2 * text : 2 * text + half] = dqall[image : image + half]
+            text_trade.start()
+
+        ost[:, 0:rows] = dqall[0:image].reshape(peers, rows, HEAD_SIZE)
+        trade.wait_recv()
+        ost[:, rows : 2 * rows] = (
+            (dkacc[0:image] * scale + xi[0].astype(F32)).astype(BF).reshape(peers, rows, HEAD_SIZE)
+        )
+        ost[:, 2 * rows : 3 * rows] = (
+            (dvacc[0:image] + xi[1].astype(F32)).astype(BF).reshape(peers, rows, HEAD_SIZE)
+        )
+        for p in range(peers):
+
+            @pl.when(me != p)
+            def _():
+                send(ost.at[p], ret.at[mine], s4.at[p], r4.at[mine], peer(p)).start()
+
+        ret[pl.ds(mine, 1)] = ost[pl.ds(me, 1)]
+
+        @pl.when(holds_text)
+        def _():
+            text_trade.wait_recv()
+            full = (seq, share, HEAD_SIZE)
+            tfin[0 : seq // 2, 0] = dqall[image : image + half].reshape(seq // 2, share, HEAD_SIZE)
+            tfin[seq // 2 : seq, 0] = ti[2 * text : 2 * text + half].reshape(seq // 2, share, HEAD_SIZE)
+            tfin[:, 1] = (
+                (dkacc[2 * image : 2 * image + text] * scale + ti[0:text].astype(F32)).astype(BF).reshape(full)
+            )
+            tfin[:, 2] = (
+                (dvacc[2 * image : 2 * image + text] + ti[text : 2 * text].astype(F32)).astype(BF).reshape(full)
+            )
+            for other in range(seq):
+
+                @pl.when(s != other)
+                def _():
+                    send(
+                        tfin.at[other], rett.at[lane_block], s5.at[other], r5.at[lane_block], (other, g)
+                    ).start()
+
+            rett[pl.ds(lane_block, 1)] = tfin[pl.ds(s, 1)]
+
+    for j in range(group):
+
+        @pl.when(s != first + c * group + j)
+        def _():
+            send(tfin.at[0], rett.at[j], s5.at[0], r5.at[j], partner).wait_recv()
+
+        cols = slice(j * HEAD_SIZE, (j + 1) * HEAD_SIZE)
+        dqt_ref[:, cols] = rett[j, 0]
+        dkt_ref[:, cols] = rett[j, 1]
+        dvt_ref[:, cols] = rett[j, 2]
+
+    for h in range(heads):
+
+        @pl.when(me != home_peer(h))
+        def _():
+            send(ost.at[0], ret.at[h], s4.at[0], r4.at[h], partner).wait_recv()
+
+        cols = slice(h * HEAD_SIZE, (h + 1) * HEAD_SIZE)
+        dq_ref[:, cols] = ret[h, 0:rows]
+        dk_ref[:, cols] = ret[h, rows : 2 * rows]
+        dv_ref[:, cols] = ret[h, 2 * rows : 3 * rows]
+
+    for h in range(heads):
+
+        @pl.when(me != home_peer(h))
+        def _():
+            first_send(h).wait_send()
+
+    @pl.when(is_head)
+    def _():
+        send(recv.at[:, pl.ds(0, 2 * rows)], kv2, s2.at[0], r2.at[0], partner).wait_send()
+        send(xo, xi, s3.at[0], r3.at[0], partner).wait_send()
+        for p in range(peers):
+
+            @pl.when(me != p)
+            def _():
+                send(ost.at[p], ret.at[mine], s4.at[p], r4.at[mine], peer(p)).wait_send()
+
+    @pl.when(takes_text)
+    def _():
+        send(to, ti, s3.at[1], r3.at[1], partner).wait_send()
+
+    @pl.when(holds_text)
+    def _():
+        for copy in text_copies():
+            copy.wait_send()
+        for other in range(seq):
+
+            @pl.when(s != other)
+            def _():
+                send(
+                    tfin.at[other], rett.at[lane_block], s5.at[other], r5.at[lane_block], (other, g)
+                ).wait_send()
+
+
+def whole_heads(
+    seq,
+    head,
+    image_input_rows,
+    adapter_down_weight,
+    adapter_up_weight,
+    image_query_rows,
+    image_key_rows,
+    image_value_codes,
+    value_fraction,
+    value_step_sizes,
+    timestep_group,
+    timestep,
+    image_output_grad,
+    text_query_rows,
+    text_key_rows,
+    text_value_rows,
+    text_output_grad,
+):
+    rows, width = image_query_rows.shape
+    text, text_width = text_query_rows.shape
+    heads, group = width // HEAD_SIZE, text_width // HEAD_SIZE
+    peers = seq * head // 2
+    image, share = peers * rows, text // seq
+    keys = 2 * image + text
+    slot_index = jnp.sum(
+        jnp.where(
+            jnp.arange(timestep_group.shape[0], dtype=jnp.int32) == timestep[0], timestep_group, 0
+        )
+    )
+    slot_rows = jnp.arange(value_step_sizes.shape[0], dtype=jnp.int32) == slot_index
+    step_row = jnp.sum(jnp.where(slot_rows[:, None], value_step_sizes, 0.0), axis=0)
+    step_lanes = jnp.repeat(step_row, HEAD_SIZE)[None, :]
+    vmem = pl.BlockSpec(memory_space=pltpu.VMEM)
+    sems = pltpu.SemaphoreType.DMA
+    dq_img, dk_img, dv_quant, dq_txt, dk_txt, dv_txt = pl.pallas_call(
+        functools.partial(attention_kernel, seq, head),
+        out_shape=[jax.ShapeDtypeStruct((rows, width), BF)] * 3
+        + [jax.ShapeDtypeStruct((share, text_width), BF)] * 3,
+        in_specs=[vmem] * 9,
+        out_specs=[vmem] * 6,
+        scratch_shapes=[
+            pltpu.VMEM((heads, 4 * rows, HEAD_SIZE), BF),
+            pltpu.VMEM((peers, 4 * rows, HEAD_SIZE), BF),
+            pltpu.VMEM((peers, 2 * rows, HEAD_SIZE), BF),
+            pltpu.VMEM((2, text, HEAD_SIZE), BF),
+            pltpu.VMEM((2, text // 2, HEAD_SIZE), BF),
+            pltpu.VMEM((keys, HEAD_SIZE), BF),
+            pltpu.VMEM((HEAD_SIZE, keys), BF),
+            pltpu.VMEM((keys, HEAD_SIZE), BF),
+            pltpu.VMEM((image + text // 2, HEAD_SIZE), BF),
+            pltpu.VMEM((image + text // 2, HEAD_SIZE), BF),
+            pltpu.VMEM((image + text // 2, HEAD_SIZE), BF),
+            pltpu.VMEM((keys, HEAD_SIZE), F32),
+            pltpu.VMEM((keys, HEAD_SIZE), F32),
+            pltpu.VMEM((2, image, HEAD_SIZE), BF),
+            pltpu.VMEM((2, image, HEAD_SIZE), BF),
+            pltpu.VMEM((2 * text + text // 2, HEAD_SIZE), BF),
+            pltpu.VMEM((2 * text + text // 2, HEAD_SIZE), BF),
+            pltpu.VMEM((peers, 3 * rows, HEAD_SIZE), BF),
+            pltpu.VMEM((heads, 3 * rows, HEAD_SIZE), BF),
+            pltpu.VMEM((seq, 3, share, HEAD_SIZE), BF),
+            pltpu.VMEM((group, 3, share, HEAD_SIZE), BF),
+            sems((heads,)),
+            sems((peers,)),
+            sems((1,)),
+            sems((1,)),
+            sems((4,)),
+            sems((4,)),
+            sems((2,)),
+            sems((2,)),
+            sems((peers,)),
+            sems((heads,)),
+            sems((seq,)),
+            sems((group,)),
+        ],
+        compiler_params=pltpu.CompilerParams(
+            collective_id=0, has_side_effects=True, vmem_limit_bytes=48 * 1024 * 1024
+        ),
+        name="whole_heads",
+    )(
+        image_query_rows,
+        image_key_rows,
+        image_value_codes,
+        image_output_grad,
+        text_query_rows,
+        text_key_rows,
+        text_value_rows,
+        text_output_grad,
+        step_lanes,
+    )
+    inside = jnp.abs(image_value_codes) < QMAX
+    lsq_term = jnp.where(
+        inside, -value_fraction.astype(jnp.float32), image_value_codes.astype(jnp.float32)
+    )
+    image_value_grad = jnp.where(inside, dv_quant, jnp.zeros_like(dv_quant))
+    lowrank_gradient = dot(image_value_grad, adapter_up_weight, NT).astype(BF)
+    part_down = jnp.einsum(
+        "td,tr->dr", image_input_rows, lowrank_gradient, preferred_element_type=jnp.float32
+    )
+    lowrank_input = dot(image_input_rows, adapter_down_weight).astype(BF)
+    part_up = jnp.einsum(
+        "tr,tw->rw", lowrank_input, image_value_grad, preferred_element_type=jnp.float32
+    )
+    token_terms = (dv_quant.astype(jnp.float32) * lsq_term).reshape(rows, heads, HEAD_SIZE)
+    total_down, total_up, step_sums = lax.psum(
+        (part_down, part_up, jnp.sum(token_terms, axis=(0, 2))), ("seq", "head")
+    )
+    grad_steps = jnp.where(slot_rows[:, None], step_sums[None, :], 0.0) * (QMAX ** (-0.5) * unscale)
+    return (
+        dq_img,
+        dk_img,
+        image_value_grad,
+        dq_txt,
+        dk_txt,
+        dv_txt,
+        total_down * unscale,
+        total_up * unscale,
+        grad_steps,
+    )
+
+
+def pick(mesh):
+    seq, head = mesh.shape["seq"], mesh.shape["head"]
+
+    def chosen(*arguments):
+        rows, width = arguments[3].shape
+        text, text_width = arguments[11].shape
+        pair = 2 * text_width // HEAD_SIZE
+        fits = (
+            head % 2 == 0
+            and seq % 2 == 0
+            and seq >= pair
+            and rows % 16 == 0
+            and text % (seq * 16) == 0
+            and (seq * head // 2 * rows) % (text // 2) == 0
+            and (seq * head * rows + text) * HEAD_SIZE <= 1 << 18
+        )
+        if fits:
+            return whole_heads(seq, head, *arguments)
+        return on_device(*arguments)
+
+    return chosen
+
+
 def solution(mesh):
     placed = (
         P(("seq", "head"), None),
@@ -253,7 +712,7 @@
         P(None, "head"),
     )
     return jax.shard_map(
-        on_device,
+        pick(mesh),
         mesh=mesh,
         in_specs=placed,
         out_specs=(

time: 425 us -> 207 us (0.49)
  blocking collectives: 169 us -> 47 us
  waiting for transfers between devices: 144 us -> 91.1 us
  Pallas kernels: 0 us -> 32.1 us
  starting transfers between devices: 25.1 us -> 0.04 us
  matrix products: 25.5 us -> 2.73 us
  local copies, waits for them, and re-layouts: 32.9 us -> 12.6 us
  other arithmetic: 11.3 us -> 5.87 us
    all_gather x4 -> x0, blocking collectives: 129 us -> none  [the longest x1 34.3 us: on_device(): lax.all_gather(key_img, 'seq', axis=0, tiled=True)]
    reduce_scatter x2 -> x0, waiting for transfers between devices: 47.4 us -> none  [the longest x1 47.4 us: on_device(): lax.psum_scatter(join_heads(text_value), 'seq', scatter_dimension=0, tile...]
    pallas_call x0 -> x1, Pallas kernels: none -> 32.1 us  [whole_heads(): pl.pallas_call(functools.partial(attention_kernel, seq, head), out_shape=...]
    all_to_all x7 -> x0, starting transfers between devices: 24.9 us -> none  [the longest x1 4.24 us: on_device(): lax.all_to_all(image_query_rows, 'head', split_axis=1, concat_axis=0, til...]
    dot_general x13 -> x2, matrix products: 25.5 us -> 2.73 us  [the longest x1 1.43 us: whole_heads(): jnp.einsum('td,tr->dr', image_input_rows, lowrank_gradient, preferred_ele...]
    convert_element_type x6 -> x0, local copies, waits for them, and re-layouts: 7.47 us -> none  [the longest x1 2.41 us: on_device(): lax.all_gather(query_local.astype(jnp.float32), 'seq', axis=0, tiled=True)]
    all_to_all x8 -> x0, local copies, waits for them, and re-layouts: 7.41 us -> none  [the longest x1 1.64 us: on_device(): lax.all_to_all(image_query_rows, 'head', split_axis=1, concat_axis=0, til...]
    unnamed x66 -> x39, local copies, waits for them, and re-layouts: 5.51 us -> 12.6 us
  transfers between devices with their start and end apart: 12 -> 1, of which waited for: 4 -> 1; matrix products, arithmetic and copies ran while one was open for 15% -> 0% of each run, Pallas kernels for 0% -> 0%
where the time goes in v1:
time: 207 us; the launch traced here: 206 us
  waiting for transfers between devices  91.1 us (44%)
  blocking collectives  47 us (23%)
  Pallas kernels  32.1 us (16%)
  between operations  14.8 us (7%)
  local copies, waits for them, and re-layouts  12.6 us (6%)
  other arithmetic  5.87 us (3%)
  matrix products  2.73 us (1%)
    psum x1, waiting for transfers between devices, whole_heads(): lax.psum((part_down, part_up, jnp.sum(token_terms, axis=(0, 2))), ('seq',...  91 us
    psum x1, blocking collectives, whole_heads(): lax.psum((part_down, part_up, jnp.sum(token_terms, axis=(0, 2))), ('seq',...  47 us
    pallas_call x1, Pallas kernels, whole_heads(): pl.pallas_call(functools.partial(attention_kernel, seq, head), out_shape=...  32.1 us
    unnamed x39, local copies, waits for them, and re-layouts  12.6 us
  transfers between devices with their start and end apart: 1, of which 1 were waited for; matrix products, arithmetic and copies ran while one was open for 0% of the time, Pallas kernels for 0%

profile of v1, /device:TPU:0, one launch (start us, length us, event | category | flops | bytes accessed | tf_op | source)
XLA Modules:
  0.0 206.3 jit_solution(729154892544318185)
XLA Ops:
  7.9 1.3 select_reduce_fusion.1
  9.3 0.6 iota_compare_fusion.1
  10.1 0.9 copy-done.1
  11.0 1.0 copy-done.3
  12.0 1.0 copy-done.4
  13.0 1.0 copy-done.5
  14.0 1.0 copy-done.6
  15.0 0.9 copy-done.7
  15.9 0.9 copy-done.8
  16.8 0.9 copy-done.9
  17.7 32.1 %whole_heads.1 = (bf16[32,1536]{1,0:T(8,128)(2,1)S(1)}, bf16[32,1536]{1,0:T(8,128)(2,1)S(1)}, bf16[32,1536]{1,0:T(8,128)(2,1)S(1)}, bf16[64,384]{1,0:T(8,128)(2,...) custom-call(bf16[32,1536]{1,0:T(8,128)(2,1)S(1)} %copy-done.7, bf16[32,1536]{1,0:T(8,128)(2,1)S(1)} %copy-done.8, ...), custom_call_target="tpu_custom_call" | custom-call | tf_op jit(solution)/shard_map/whole_heads/pallas_call | solution.py:586
  49.9 0.9 copy-done.11
  50.8 1.3 fusion
  52.1 1.4 convolution_bitcast_fusion
  53.5 0.9 copy-done.2
  54.7 47.0 %psum.23 = f32[12]{0:T(128)S(1)} all-reduce(f32[12]{0:T(128)S(1)} %bitcast_reduce_fusion), channel_id=1, replica_groups=mesh['seq'=8,'head'=4] {'seq','head'}, use_global_device_ids=true, to_apply=%region_6.7 | all-reduce | flops 12 | bytes 96 | tf_op jit(solution)/shard_map/psum | solution.py:656
  101.7 0.7 select_multiply_fusion
  102.4 91.0 %all-reduce.3.cloned.1.call-done = (f32[3072,64]{0,1:T(8,128)}, f32[64,1536]{1,0:T(8,128)}) async-done(((f32[3072,64]{0,1:T(8,128)}, f32[64,1536]{1,0:T(8,128)}), (f32[3072,64]{0,1:T(8,128)}, f32[64,1536]{1,0:T(8,128)})) %all-reduce.3.cloned.1.call-update) | async-done | bytes 1179664 | tf_op jit(solution)/shard_map/psum | solution.py:656
  193.4 2.1 %broadcast_multiply_fusion = f32[3072,64]{0,1:T(8,128)} fusion(f32[3072,64]{0,1:T(8,128)} %get-tuple-element.21), kind=kLoop, calls=%fused_computation.4 | loop fusion | flops 196608 | bytes 1572864 | tf_op jit(solution)/shard_map/mul | solution.py:667
  195.5 0.8 broadcast_multiply_fusion.1
  196.3 0.6 copy.35
  197.0 0.6 copy.36
  197.6 0.6 copy.37
  198.2 0.6 copy.38
  (31 shorter events, 1.2 us)
Async XLA Ops:
  7.2 42.7 %copy-start = (bf16[3072,64]{0,1:T(8,128)(2,1)S(1)}, bf16[3072,64]{0,1:T(8,128)(2,1)}, u32[]{:S(2)}) copy-start(bf16[3072,64]{0,1:T(8,128)(2,1)} %param.16) | copy-start | bytes 1179652
  7.2 186.2 %all-reduce.3.cloned.1.call-start = ((), (), s32[]{:S(2)}) async-start(), calls=%async_computation | async-start | bytes 2359296 | tf_op jit(solution)/shard_map/psum | solution.py:656
  7.9 2.0 copy-start.15
  10.1 0.9 copy-start.1
  11.0 1.0 copy-start.3
  12.0 1.0 copy-start.4
  13.0 1.0 copy-start.5
  14.0 1.0 copy-start.6
  15.0 0.9 copy-start.7
  15.9 0.9 copy-start.8
  16.8 0.9 copy-start.9
  49.8 0.9 copy-start.11
  50.8 1.3 copy-start.10
  50.8 1.3 copy-start.13
  53.5 0.9 copy-start.2
  53.5 1.0 copy-start.14
  193.4 2.1 %copy-start.12 = (f32[64,1536]{1,0:T(8,128)S(1)}, f32[64,1536]{1,0:T(8,128)}, u32[]{:S(2)}) copy-start(f32[64,1536]{1,0:T(8,128)} %get-tuple-element.22) | copy-start | bytes 1179652
Sparse Core Ops, SparseCore 0:
  53.6 139.7 all-reduce.2

commit v2 on v1

--- a/solution.py
+++ b/solution.py
@@ -251,21 +251,38 @@
 def attention_kernel(
     seq,
     head,
-    q_ref,
-    k_ref,
-    code_ref,
-    do_ref,
-    tq_ref,
-    tk_ref,
-    tv_ref,
-    tdo_ref,
+    q_in,
+    k_in,
+    code_in,
+    do_in,
+    tq_in,
+    tk_in,
+    tv_in,
+    tdo_in,
+    x_in,
+    frac_in,
+    up_in,
+    down_in,
     step_ref,
+    group_ref,
+    time_ref,
     dq_ref,
     dk_ref,
     dv_ref,
     dqt_ref,
     dkt_ref,
     dvt_ref,
+    down_ref,
+    up_ref,
+    steps_ref,
+    q_ref,
+    k_ref,
+    code_ref,
+    do_ref,
+    x_ref,
+    frac_ref,
+    upw_ref,
+    downw_ref,
     stage,
     recv,
     kv2,
@@ -287,6 +304,19 @@
     ret,
     tfin,
     rett,
+    xlow_out,
+    xlow_in,
+    xst,
+    xcol,
+    up_out,
+    up_in2,
+    up_all,
+    low_out,
+    low_in,
+    red_out,
+    red_in,
+    gath,
+    li,
     s1,
     r1,
     s2,
@@ -299,19 +329,38 @@
     r4,
     s5,
     r5,
+    s6,
+    r6,
+    s7,
+    r7,
+    s8,
+    r8,
+    s9,
+    r9,
+    s10,
+    r10,
+    s11,
+    r11,
+    s12,
+    r12,
 ):
     rows = q_ref.shape[0]
     heads = q_ref.shape[1] // HEAD_SIZE
-    text = tq_ref.shape[0]
+    text = tq_in.shape[0]
     half = text // 2
     planes = head // 2
     peers = seq * planes
-    group = tq_ref.shape[1] // HEAD_SIZE
+    group = tq_in.shape[1] // HEAD_SIZE
     pair = 2 * group
     first = (seq - pair) // 2
     image = peers * rows
     share = text // seq
     scale = HEAD_SIZE ** (-0.5)
+    rank = upw_ref.shape[0]
+    wide = x_ref.shape[1] // seq
+    part = rank // head
+    hrank = rank // 2
+    hrows = rows // 2
 
     s = lax.axis_index("seq")
     g = lax.axis_index("head")
@@ -327,28 +376,49 @@
     lane_block = lax.rem(slot, group)
 
     def peer(p):
-        return (p // planes, (p % planes) * 2 + c)
+        return (p // planes, lax.rem(p, planes) * 2 + c)
 
     def home(h):
-        return (first + h % pair, (h // pair) * 2 + c)
+        return (first + lax.rem(h, pair), (h // pair) * 2 + c)
 
     def home_peer(h):
-        return (first + h % pair) * planes + h // pair
+        return (first + lax.rem(h, pair)) * planes + h // pair
 
     def send(src, dst, ssem, rsem, to_id):
         return pltpu.make_async_remote_copy(
             src_ref=src, dst_ref=dst, send_sem=ssem, recv_sem=rsem, device_id=to_id, device_id_type=MESH
         )
 
+    loads = [
+        pltpu.make_async_copy(src, dst, li.at[i])
+        for i, (src, dst) in enumerate(
+            (
+                (k_in, k_ref),
+                (code_in, code_ref),
+                (q_in, q_ref),
+                (do_in, do_ref),
+                (x_in, x_ref),
+                (down_in, downw_ref),
+                (up_in, upw_ref),
+                (frac_in, frac_ref),
+            )
+        )
+    ]
+    for load in loads:
+        load.start()
+
     barrier = pltpu.get_barrier_semaphore()
-    for p in range(peers):
-
-        @pl.when(me != p)
-        def _():
-            pl.semaphore_signal(barrier, inc=1, device_id=peer(p), device_id_type=MESH)
-
-    pl.semaphore_signal(barrier, inc=1, device_id=partner, device_id_type=MESH)
-
+    for i in range(1, peers):
+        pl.semaphore_signal(
+            barrier, inc=1, device_id=peer(lax.rem(me + i, peers)), device_id_type=MESH
+        )
+    for other in range(planes):
+        pl.semaphore_signal(
+            barrier, inc=1, device_id=(s, other * 2 + 1 - c), device_id_type=MESH
+        )
+
+    for load in loads[:4]:
+        load.wait()
     for h in range(heads):
         cols = slice(h * HEAD_SIZE, (h + 1) * HEAD_SIZE)
         stage[h, 0:rows] = k_ref[:, cols]
@@ -356,7 +426,7 @@
         stage[h, 2 * rows : 3 * rows] = q_ref[:, cols]
         stage[h, 3 * rows : 4 * rows] = do_ref[:, cols]
 
-    pl.semaphore_wait(barrier, peers)
+    pl.semaphore_wait(barrier, peers - 1 + planes)
 
     def first_send(h):
         return send(stage.at[h], recv.at[me], s1.at[h], r1.at[me], home(h))
@@ -364,35 +434,77 @@
     def first_recv(p):
         return send(stage.at[0], recv.at[p], s1.at[0], r1.at[p], partner)
 
-    for h in range(heads):
+    for i in range(heads):
+        h = lax.rem(me + i, heads)
 
         @pl.when(me != home_peer(h))
         def _():
             first_send(h).start()
 
+    def text_sources():
+        cols = pl.ds(pl.multiple_of(lane_block * HEAD_SIZE, HEAD_SIZE), HEAD_SIZE)
+        return cols, pl.ds(0, half), pl.ds(half, half)
+
     def text_copies():
-        cols = pl.ds(pl.multiple_of(lane_block * HEAD_SIZE, HEAD_SIZE), HEAD_SIZE)
-        low = pl.ds(half, half)
+        cols, _, low = text_sources()
         return (
-            send(tk_ref.at[:, cols], tkv.at[0], st.at[0], rt.at[0], partner),
-            send(tv_ref.at[:, cols], tkv.at[1], st.at[1], rt.at[1], partner),
-            send(tq_ref.at[low, cols], tqd.at[0], st.at[2], rt.at[2], partner),
-            send(tdo_ref.at[low, cols], tqd.at[1], st.at[3], rt.at[3], partner),
+            send(tk_in.at[:, cols], tkv.at[0], st.at[0], rt.at[0], partner),
+            send(tv_in.at[:, cols], tkv.at[1], st.at[1], rt.at[1], partner),
+            send(tq_in.at[low, cols], tqd.at[0], st.at[2], rt.at[2], partner),
+            send(tdo_in.at[low, cols], tqd.at[1], st.at[3], rt.at[3], partner),
+        )
+
+    def text_loads():
+        cols, high, _ = text_sources()
+        return (
+            pltpu.make_async_copy(tk_in.at[:, cols], tkv.at[0], li.at[8]),
+            pltpu.make_async_copy(tv_in.at[:, cols], tkv.at[1], li.at[9]),
+            pltpu.make_async_copy(tq_in.at[high, cols], tqd.at[0], li.at[10]),
+            pltpu.make_async_copy(tdo_in.at[high, cols], tqd.at[1], li.at[11]),
         )
 
     @pl.when(holds_text)
     def _():
-        for copy in text_copies():
+        for copy in text_copies() + text_loads():
             copy.start()
-        cols = pl.ds(pl.multiple_of(lane_block * HEAD_SIZE, HEAD_SIZE), HEAD_SIZE)
-        kall[2 * image : 2 * image + text] = tk_ref[:, cols]
-        vall[2 * image : 2 * image + text] = tv_ref[:, cols]
-        qall[image : image + half] = tq_ref[0:half, cols]
-        doall[image : image + half] = tdo_ref[0:half, cols]
+
+    for load in loads[4:6]:
+        load.wait()
+    for t in range(seq):
+        xst[t] = x_ref[:, t * wide : (t + 1) * wide]
+
+    def column_send(t):
+        return send(xst.at[t], xcol.at[s], s6.at[t], r6.at[s], (t, g))
+
+    for i in range(1, seq):
+        column_send(lax.rem(s + i, seq)).start()
+    xcol[pl.ds(s, 1)] = xst[pl.ds(s, 1)]
+
+    xlow = dot(x_ref[...], downw_ref[...])
+    xlow_out[...] = jnp.concatenate([xlow[0:hrows], xlow[hrows:rows]], axis=1).astype(BF)
+
+    def low_send(h):
+        return send(xlow_out, xlow_in.at[me], s7.at[h], r7.at[me], home(h))
+
+    for i in range(heads):
+        h = lax.rem(me + i, heads)
+
+        @pl.when(me != home_peer(h))
+        def _():
+            low_send(h).start()
+
+    for load in loads[6:8]:
+        load.wait()
+
+    def up_send(p):
+        return send(
+            up_out.at[c], up_all.at[mine, c], s9.at[p], r9.at[mine], peer(p)
+        )
 
     @pl.when(is_head)
     def _():
         recv[pl.ds(me, 1)] = stage[pl.ds(mine, 1)]
+        xlow_in[pl.ds(me, 1)] = xlow_out[...].reshape(1, hrows, HEAD_SIZE)
         for p in range(peers):
 
             @pl.when(me != p)
@@ -401,7 +513,7 @@
 
         swap = send(recv.at[:, pl.ds(0, 2 * rows)], kv2, s2.at[0], r2.at[0], partner)
         swap.start()
-        step = step_ref[:, pl.ds(pl.multiple_of(mine * HEAD_SIZE, HEAD_SIZE), HEAD_SIZE)]
+        step = step_ref[group_ref[time_ref[0]], mine]
 
         def dequant(codes):
             return (codes.reshape(image, HEAD_SIZE).astype(F32) * step).astype(BF)
@@ -415,11 +527,16 @@
         def _():
             for copy in text_copies():
                 copy.wait_recv()
-            kall[2 * image : 2 * image + text] = tkv[0]
-            vall[2 * image : 2 * image + text] = tkv[1]
-            qall[image : image + half] = tqd[0]
-            doall[image : image + half] = tqd[1]
-
+
+        @pl.when(holds_text)
+        def _():
+            for copy in text_loads():
+                copy.wait()
+
+        kall[2 * image : 2 * image + text] = tkv[0]
+        vall[2 * image : 2 * image + text] = tkv[1]
+        qall[image : image + half] = tqd[0]
+        doall[image : image + half] = tqd[1]
         swap.wait_recv()
         kall[image : 2 * image] = kv2[:, 0:rows].reshape(image, HEAD_SIZE)
         vall[image : 2 * image] = dequant(kv2[:, rows : 2 * rows])
@@ -463,13 +580,29 @@
         ost[:, 2 * rows : 3 * rows] = (
             (dvacc[0:image] + xi[1].astype(F32)).astype(BF).reshape(peers, rows, HEAD_SIZE)
         )
+        for i in range(1, peers):
+            p = lax.rem(me + i, peers)
+            send(ost.at[p], ret.at[mine], s4.at[p], r4.at[mine], peer(p)).start()
+
+        ret[pl.ds(mine, 1)] = ost[pl.ds(me, 1)]
+
         for p in range(peers):
 
             @pl.when(me != p)
             def _():
-                send(ost.at[p], ret.at[mine], s4.at[p], r4.at[mine], peer(p)).start()
-
-        ret[pl.ds(mine, 1)] = ost[pl.ds(me, 1)]
+                send(xlow_out, xlow_in.at[p], s7.at[0], r7.at[p], partner).wait_recv()
+
+        codes = recv[:, rows : 2 * rows]
+        kept = jnp.where(jnp.abs(codes.astype(F32)) < QMAX, ost[:, 2 * rows : 3 * rows].astype(F32), 0.0)
+        kept = kept.astype(BF)
+        low_rows = xlow_in[...].reshape(peers * hrows, HEAD_SIZE).T
+        early = dot(low_rows, kept[:, 0:hrows].reshape(peers * hrows, HEAD_SIZE))
+        late = dot(low_rows, kept[:, hrows:rows].reshape(peers * hrows, HEAD_SIZE))
+        part_up = (early[0:rank] + late[rank : 2 * rank]).reshape(2, hrank, HEAD_SIZE)
+        up_out32 = up_in2.at[0]
+        up_out32[...] = part_up
+        up_trade = send(up_in2.at[0, 1 - c], up_in2.at[1, 0], s8.at[0], r8.at[0], partner)
+        up_trade.start()
 
         @pl.when(holds_text)
         def _():
@@ -483,15 +616,58 @@
             tfin[:, 2] = (
                 (dvacc[2 * image : 2 * image + text] + ti[text : 2 * text].astype(F32)).astype(BF).reshape(full)
             )
-            for other in range(seq):
-
-                @pl.when(s != other)
-                def _():
-                    send(
-                        tfin.at[other], rett.at[lane_block], s5.at[other], r5.at[lane_block], (other, g)
-                    ).start()
+            for i in range(1, seq):
+                other = lax.rem(s + i, seq)
+                send(
+                    tfin.at[other], rett.at[lane_block], s5.at[other], r5.at[lane_block], (other, g)
+                ).start()
 
             rett[pl.ds(lane_block, 1)] = tfin[pl.ds(s, 1)]
+
+        up_trade.wait_recv()
+        up_out[pl.ds(c, 1)] = (
+            (up_in2[pl.ds(0, 1), pl.ds(c, 1)] + up_in2[pl.ds(1, 1), pl.ds(0, 1)]) * unscale
+        ).astype(BF).reshape(1, hrank, HEAD_SIZE)
+        for i in range(1, peers):
+            up_send(lax.rem(me + i, peers)).start()
+        up_all[pl.ds(mine, 1), pl.ds(c, 1)] = up_out[pl.ds(c, 1)].reshape(1, 1, hrank, HEAD_SIZE)
+
+    low = jnp.zeros((rows, rank), F32)
+    lane = lax.broadcasted_iota(jnp.int32, (1, HEAD_SIZE), 1)
+    step_terms = jnp.zeros((1, HEAD_SIZE), F32)
+    for h in range(heads):
+
+        @pl.when(me != home_peer(h))
+        def _():
+            send(ost.at[0], ret.at[h], s4.at[0], r4.at[h], partner).wait_recv()
+
+        cols = slice(h * HEAD_SIZE, (h + 1) * HEAD_SIZE)
+        codes = code_ref[:, cols]
+        inside = jnp.abs(codes) < QMAX
+        value_grad = ret[h, 2 * rows : 3 * rows].astype(F32)
+        kept = jnp.where(inside, value_grad, 0.0).astype(BF)
+        lsq_term = jnp.where(inside, -frac_ref[:, cols].astype(F32), codes.astype(F32))
+        total = jnp.sum(value_grad * lsq_term)
+        step_terms = step_terms + jnp.where(lane == h, total, 0.0)
+        low = low + dot(kept, upw_ref[:, cols], NT)
+        dq_ref[:, cols] = ret[h, 0:rows]
+        dk_ref[:, cols] = ret[h, rows : 2 * rows]
+        dv_ref[:, cols] = kept
+
+    step_high = step_terms.astype(BF).astype(F32)
+    step_low = step_terms - step_high
+    row_at = lax.broadcasted_iota(jnp.int32, (rows, rank), 0)
+    beside = jnp.where(
+        row_at == 0, step_high[:, 0:rank], jnp.where(row_at == 1, step_low[:, 0:rank], 0.0)
+    )
+    low_out[...] = jnp.concatenate([low, beside], axis=1).astype(BF)
+
+    def tile_send(t):
+        return send(low_out, low_in.at[s], s10.at[t], r10.at[s], (t, g))
+
+    for i in range(1, seq):
+        tile_send(lax.rem(s + i, seq)).start()
+    low_in[pl.ds(s, 1)] = low_out[...].reshape(1, rows, HEAD_SIZE)
 
     for j in range(group):
 
@@ -504,32 +680,125 @@
         dkt_ref[:, cols] = rett[j, 1]
         dvt_ref[:, cols] = rett[j, 2]
 
+    for t in range(seq):
+
+        @pl.when(s != t)
+        def _():
+            send(xst.at[0], xcol.at[t], s6.at[0], r6.at[t], partner).wait_recv()
+            send(low_out, low_in.at[t], s10.at[0], r10.at[t], partner).wait_recv()
+
+    tiles = low_in[...]
+    flat = tiles.reshape(seq * rows, HEAD_SIZE).T
+    block = dot(flat, xcol[...].reshape(seq * rows, wide))[0:rank]
+    step_group = jnp.sum(
+        jnp.sum(tiles[:, 0:2].astype(F32), axis=0), axis=0, keepdims=True
+    )
+    for other in range(head):
+        red_out[other, 0:part] = block[other * part : (other + 1) * part]
+        red_out[other, part : part + 8, 0:HEAD_SIZE] = jnp.broadcast_to(step_group, (8, HEAD_SIZE))
+        red_out[other, part : part + 8, HEAD_SIZE:wide] = jnp.zeros((8, wide - HEAD_SIZE), F32)
+
+    def reduce_send(other):
+        return send(red_out.at[other], red_in.at[g], s11.at[other], r11.at[g], (s, other))
+
+    for i in range(1, head):
+        reduce_send(lax.rem(g + i, head)).start()
+    red_in[pl.ds(g, 1)] = red_out[pl.ds(g, 1)]
+    for other in range(head):
+
+        @pl.when(g != other)
+        def _():
+            send(red_out.at[0], red_in.at[other], s11.at[0], r11.at[other], partner).wait_recv()
+
+    summed = jnp.sum(red_in[...], axis=0)
+    gath[pl.ds(y, 1), pl.ds(c, 1), pl.ds(s, 1)] = (
+        (summed[0:part] * unscale).astype(BF).reshape(1, 1, 1, part, wide)
+    )
+
+    def row_send(t):
+        return send(
+            gath.at[y, c, s], gath.at[y, c, s], s12.at[t], r12.at[s], (t, g)
+        )
+
+    def plane_send(i):
+        to_plane = lax.rem(y + i, planes)
+        return send(
+            gath.at[y, c], gath.at[y, c], s12.at[seq + i], r12.at[seq + y], (s, to_plane * 2 + c)
+        )
+
+    def core_send():
+        return send(gath.at[:, c], gath.at[:, c], s12.at[seq], r12.at[seq + planes], partner)
+
+    def core_up_send():
+        return send(up_all.at[:, c], up_all.at[:, c], s8.at[1], r8.at[1], partner)
+
+    for i in range(1, seq):
+        row_send(lax.rem(s + i, seq)).start()
+
+    slot_index = group_ref[time_ref[0]]
+    step_row = summed[part : part + 1, HEAD_SIZE // 2 : HEAD_SIZE // 2 + heads] * (QMAX ** (-0.5) * unscale)
+    slots = steps_ref.shape[0]
+    slot_at = lax.broadcasted_iota(jnp.int32, (slots, heads), 0)
+    steps_ref[...] = jnp.where(slot_at == slot_index, jnp.broadcast_to(step_row, (slots, heads)), 0.0)
+
     for h in range(heads):
 
         @pl.when(me != home_peer(h))
         def _():
-            send(ost.at[0], ret.at[h], s4.at[0], r4.at[h], partner).wait_recv()
-
+            send(up_out.at[0], up_all.at[h, c], s9.at[0], r9.at[h], partner).wait_recv()
+
+    core_up_send().start()
+
+    for t in range(seq):
+
+        @pl.when(s != t)
+        def _():
+            send(gath.at[y, c, t], gath.at[y, c, t], s12.at[0], r12.at[t], partner).wait_recv()
+
+    for i in range(1, planes):
+        plane_send(i).start()
+    for i in range(1, planes):
+        from_plane = lax.rem(y + i, planes)
+        send(
+            gath.at[from_plane, c], gath.at[from_plane, c], s12.at[seq + i], r12.at[seq + from_plane], partner
+        ).wait_recv()
+    core_send().start()
+    send(up_all.at[:, 1 - c], up_all.at[:, 1 - c], s8.at[1], r8.at[1], partner).wait_recv()
+    for h in range(heads):
         cols = slice(h * HEAD_SIZE, (h + 1) * HEAD_SIZE)
-        dq_ref[:, cols] = ret[h, 0:rows]
-        dk_ref[:, cols] = ret[h, rows : 2 * rows]
-        dv_ref[:, cols] = ret[h, 2 * rows : 3 * rows]
+        up_ref[:, cols] = up_all[h].reshape(rank, HEAD_SIZE).astype(F32)
+    send(gath.at[:, 1 - c], gath.at[:, 1 - c], s12.at[seq], r12.at[seq + planes], partner).wait_recv()
+    for t in range(seq):
+        down_ref[t * wide : (t + 1) * wide] = gath[:, :, t].reshape(rank, wide).astype(F32).T
 
     for h in range(heads):
 
         @pl.when(me != home_peer(h))
         def _():
             first_send(h).wait_send()
+            low_send(h).wait_send()
+
+    for i in range(1, seq):
+        t = lax.rem(s + i, seq)
+        column_send(t).wait_send()
+        tile_send(t).wait_send()
+        row_send(t).wait_send()
+    for i in range(1, head):
+        reduce_send(lax.rem(g + i, head)).wait_send()
+    for i in range(1, planes):
+        plane_send(i).wait_send()
+    core_send().wait_send()
+    core_up_send().wait_send()
 
     @pl.when(is_head)
     def _():
         send(recv.at[:, pl.ds(0, 2 * rows)], kv2, s2.at[0], r2.at[0], partner).wait_send()
         send(xo, xi, s3.at[0], r3.at[0], partner).wait_send()
-        for p in range(peers):
-
-            @pl.when(me != p)
-            def _():
-                send(ost.at[p], ret.at[mine], s4.at[p], r4.at[mine], peer(p)).wait_send()
+        send(up_in2.at[0, 1 - c], up_in2.at[1, 0], s8.at[0], r8.at[0], partner).wait_send()
+        for i in range(1, peers):
+            p = lax.rem(me + i, peers)
+            send(ost.at[p], ret.at[mine], s4.at[p], r4.at[mine], peer(p)).wait_send()
+            up_send(p).wait_send()
 
     @pl.when(takes_text)
     def _():
@@ -539,13 +808,11 @@
     def _():
         for copy in text_copies():
             copy.wait_send()
-        for other in range(seq):
-
-            @pl.when(s != other)
-            def _():
-                send(
-                    tfin.at[other], rett.at[lane_block], s5.at[other], r5.at[lane_block], (other, g)
-                ).wait_send()
+        for i in range(1, seq):
+            other = lax.rem(s + i, seq)
+            send(
+                tfin.at[other], rett.at[lane_block], s5.at[other], r5.at[lane_block], (other, g)
+            ).wait_send()
 
 
 def whole_heads(
@@ -573,23 +840,32 @@
     peers = seq * head // 2
     image, share = peers * rows, text // seq
     keys = 2 * image + text
-    slot_index = jnp.sum(
-        jnp.where(
-            jnp.arange(timestep_group.shape[0], dtype=jnp.int32) == timestep[0], timestep_group, 0
-        )
-    )
-    slot_rows = jnp.arange(value_step_sizes.shape[0], dtype=jnp.int32) == slot_index
-    step_row = jnp.sum(jnp.where(slot_rows[:, None], value_step_sizes, 0.0), axis=0)
-    step_lanes = jnp.repeat(step_row, HEAD_SIZE)[None, :]
+    rank, wide = adapter_up_weight.shape[0], image_input_rows.shape[1] // seq
+    planes = head // 2
     vmem = pl.BlockSpec(memory_space=pltpu.VMEM)
     sems = pltpu.SemaphoreType.DMA
-    dq_img, dk_img, dv_quant, dq_txt, dk_txt, dv_txt = pl.pallas_call(
+    hbm = pl.BlockSpec(memory_space=pl.ANY)
+    smem = pl.BlockSpec(memory_space=pltpu.SMEM)
+    return tuple(pl.pallas_call(
         functools.partial(attention_kernel, seq, head),
         out_shape=[jax.ShapeDtypeStruct((rows, width), BF)] * 3
-        + [jax.ShapeDtypeStruct((share, text_width), BF)] * 3,
-        in_specs=[vmem] * 9,
-        out_specs=[vmem] * 6,
+        + [jax.ShapeDtypeStruct((share, text_width), BF)] * 3
+        + [
+            jax.ShapeDtypeStruct(adapter_down_weight.shape, F32),
+            jax.ShapeDtypeStruct(adapter_up_weight.shape, F32),
+            jax.ShapeDtypeStruct(value_step_sizes.shape, F32),
+        ],
+        in_specs=[hbm] * 12 + [smem] * 3,
+        out_specs=[vmem] * 9,
         scratch_shapes=[
+            pltpu.VMEM((rows, width), BF),
+            pltpu.VMEM((rows, width), BF),
+            pltpu.VMEM((rows, width), jnp.int32),
+            pltpu.VMEM((rows, width), BF),
+            pltpu.VMEM(image_input_rows.shape, BF),
+            pltpu.VMEM((rows, width), BF),
+            pltpu.VMEM(adapter_up_weight.shape, BF),
+            pltpu.VMEM(adapter_down_weight.shape, BF),
             pltpu.VMEM((heads, 4 * rows, HEAD_SIZE), BF),
             pltpu.VMEM((peers, 4 * rows, HEAD_SIZE), BF),
             pltpu.VMEM((peers, 2 * rows, HEAD_SIZE), BF),
@@ -611,6 +887,19 @@
             pltpu.VMEM((heads, 3 * rows, HEAD_SIZE), BF),
             pltpu.VMEM((seq, 3, share, HEAD_SIZE), BF),
             pltpu.VMEM((group, 3, share, HEAD_SIZE), BF),
+            pltpu.VMEM((rows // 2, HEAD_SIZE), BF),
+            pltpu.VMEM((peers, rows // 2, HEAD_SIZE), BF),
+            pltpu.VMEM((seq, rows, wide), BF),
+            pltpu.VMEM((seq, rows, wide), BF),
+            pltpu.VMEM((2, rank // 2, HEAD_SIZE), BF),
+            pltpu.VMEM((2, 2, rank // 2, HEAD_SIZE), F32),
+            pltpu.VMEM((heads, 2, rank // 2, HEAD_SIZE), BF),
+            pltpu.VMEM((rows, HEAD_SIZE), BF),
+            pltpu.VMEM((seq, rows, HEAD_SIZE), BF),
+            pltpu.VMEM((head, rank // head + 8, wide), F32),
+            pltpu.VMEM((head, rank // head + 8, wide), F32),
+            pltpu.VMEM((planes, 2, seq, rank // head, wide), BF),
+            sems((12,)),
             sems((heads,)),
             sems((peers,)),
             sems((1,)),
@@ -623,9 +912,23 @@
             sems((heads,)),
             sems((seq,)),
             sems((group,)),
+            sems((seq,)),
+            sems((seq,)),
+            sems((heads,)),
+            sems((peers,)),
+            sems((2,)),
+            sems((2,)),
+            sems((peers,)),
+            sems((heads,)),
+            sems((seq,)),
+            sems((seq,)),
+            sems((head,)),
+            sems((head,)),
+            sems((seq + planes,)),
+            sems((seq + planes + 1,)),
         ],
         compiler_params=pltpu.CompilerParams(
-            collective_id=0, has_side_effects=True, vmem_limit_bytes=48 * 1024 * 1024
+            collective_id=0, has_side_effects=True, vmem_limit_bytes=56 * 1024 * 1024
         ),
         name="whole_heads",
     )(
@@ -637,37 +940,14 @@
         text_key_rows,
         text_value_rows,
         text_output_grad,
-        step_lanes,
-    )
-    inside = jnp.abs(image_value_codes) < QMAX
-    lsq_term = jnp.where(
-        inside, -value_fraction.astype(jnp.float32), image_value_codes.astype(jnp.float32)
-    )
-    image_value_grad = jnp.where(inside, dv_quant, jnp.zeros_like(dv_quant))
-    lowrank_gradient = dot(image_value_grad, adapter_up_weight, NT).astype(BF)
-    part_down = jnp.einsum(
-        "td,tr->dr", image_input_rows, lowrank_gradient, preferred_element_type=jnp.float32
-    )
-    lowrank_input = dot(image_input_rows, adapter_down_weight).astype(BF)
-    part_up = jnp.einsum(
-        "tr,tw->rw", lowrank_input, image_value_grad, preferred_element_type=jnp.float32
-    )
-    token_terms = (dv_quant.astype(jnp.float32) * lsq_term).reshape(rows, heads, HEAD_SIZE)
-    total_down, total_up, step_sums = lax.psum(
-        (part_down, part_up, jnp.sum(token_terms, axis=(0, 2))), ("seq", "head")
-    )
-    grad_steps = jnp.where(slot_rows[:, None], step_sums[None, :], 0.0) * (QMAX ** (-0.5) * unscale)
-    return (
-        dq_img,
-        dk_img,
-        image_value_grad,
-        dq_txt,
-        dk_txt,
-        dv_txt,
-        total_down * unscale,
-        total_up * unscale,
-        grad_steps,
-    )
+        image_input_rows,
+        value_fraction,
+        adapter_up_weight,
+        adapter_down_weight,
+        value_step_sizes,
+        timestep_group,
+        timestep,
+    ))
 
 
 def pick(mesh):
@@ -681,7 +961,11 @@
             head % 2 == 0
             and seq % 2 == 0
             and seq >= pair
-            and rows % 16 == 0
+            and rows % 32 == 0
+            and 2 * arguments[2].shape[0] == HEAD_SIZE
+            and width // HEAD_SIZE <= arguments[2].shape[0]
+            and arguments[2].shape[0] % (16 * head) == 0
+            and arguments[0].shape[1] % (seq * HEAD_SIZE) == 0
             and text % (seq * 16) == 0
             and (seq * head // 2 * rows) % (text // 2) == 0
             and (seq * head * rows + text) * HEAD_SIZE <= 1 << 18

time: 207 us -> 76.1 us (0.37)
  waiting for transfers between devices: 91.1 us -> 0 us
  blocking collectives: 47 us -> 0 us
  Pallas kernels: 32.1 us -> 63.8 us
  between operations: 14.8 us -> 1.37 us
  other arithmetic: 5.87 us -> 0 us
  matrix products: 2.73 us -> 0 us
  local copies, waits for them, and re-layouts: 12.6 us -> 10.2 us
    psum x1 -> x0, waiting for transfers between devices: 91 us -> none  [whole_heads(): lax.psum((part_down, part_up, jnp.sum(token_terms, axis=(0, 2))), ('seq',...]
    psum x1 -> x0, blocking collectives: 47 us -> none  [whole_heads(): lax.psum((part_down, part_up, jnp.sum(token_terms, axis=(0, 2))), ('seq',...]
    pallas_call x1, Pallas kernels: 32.1 us -> 63.8 us  [whole_heads(): pl.pallas_call(functools.partial(attention_kernel, seq, head), out_shape=...]
    unnamed x39 -> x25, local copies, waits for them, and re-layouts: 12.6 us -> 7.31 us
    mul x3 -> x0, other arithmetic: 3.56 us -> none  [the longest x1 2.12 us: whole_heads(): total_down * unscale]
    pallas_call x0 -> x1, local copies, waits for them, and re-layouts: none -> 2.85 us  [whole_heads(): pl.pallas_call(functools.partial(attention_kernel, seq, head), out_shape=...]
    dot_general x2 -> x0, matrix products: 2.73 us -> none  [the longest x1 1.43 us: whole_heads(): jnp.einsum('td,tr->dr', image_input_rows, lowrank_gradient, preferred_ele...]
  transfers between devices with their start and end apart: 1 -> 0, of which waited for: 1 -> 0; matrix products, arithmetic and copies ran while one was open for 0% -> 0% of each run, Pallas kernels for 0% -> 0%
where the time goes in v2:
time: 76.1 us; the launch traced here: 75.3 us
  Pallas kernels  63.8 us (84%)
  local copies, waits for them, and re-layouts  10.2 us (13%)
  between operations  1.37 us (2%)
    pallas_call x1, Pallas kernels, whole_heads(): pl.pallas_call(functools.partial(attention_kernel, seq, head), out_shape=...  63.8 us
    unnamed x25, local copies, waits for them, and re-layouts  7.31 us
    pallas_call x1, local copies, waits for them, and re-layouts, whole_heads(): pl.pallas_call(functools.partial(attention_kernel, seq, head), out_shape=...  2.85 us

profile of v2, /device:TPU:0, one launch (start us, length us, event | category | flops | bytes accessed | tf_op | source)
XLA Modules:
  0.0 75.3 jit_solution(11486639841439328836)
XLA Ops:
  1.3 2.2 %copy.24.down_in = bf16[3072,64]{1,0:T(8,128)(2,1)} copy(bf16[3072,64]{0,1:T(8,128)(2,1)} %param.16) | data formatting | bytes 786432 | tf_op args[1]
  3.4 63.8 %whole_heads.1 = (bf16[32,1536]{1,0:T(8,128)(2,1)}, bf16[32,1536]{1,0:T(8,128)(2,1)}, bf16[32,1536]{1,0:T(8,128)(2,1)}, bf16[64,384]{1,0:T(8,128)(2,1)}, bf16[64...) custom-call(bf16[32,1536]{1,0:T(8,128)(2,1)} %q_in.1, ...), custom_call_target="tpu_custom_call" | custom-call | tf_op jit(solution)/shard_map/whole_heads/pallas_call | solution.py:849
  67.3 0.0 copy-start.3
  67.3 0.0 copy-start.2
  67.3 0.0 copy-start.1
  67.3 0.0 copy-start.6
  67.3 0.0 copy-start.5
  67.3 0.0 copy-start.4
  67.3 0.0 copy-start
  67.3 0.0 copy-start.7
  67.3 2.9 %copy.25 = f32[3072,64]{0,1:T(8,128)} copy(f32[3072,64]{1,0:T(8,128)} %get-tuple-element.15) | data formatting | bytes 1572864 | tf_op jit(solution)/shard_map/whole_heads/pallas_call | solution.py:849
  70.2 0.0 copy-done.3
  70.2 0.6 copy.35
  70.8 0.0 copy-done.2
  70.8 0.6 copy.36
  71.5 0.0 copy-done.1
  71.5 0.6 copy.37
  72.1 0.0 copy-done.6
  72.1 0.6 copy.38
  72.8 0.0 copy-done.5
  72.8 0.6 copy.39
  73.4 0.6 copy.40
  74.0 0.7 copy.41
  74.8 0.6 copy.42
  (3 shorter events, 0.0 us)
Async XLA Ops:
  67.3 2.9 %copy-start.3 = (bf16[32,1536]{1,0:T(8,128)(2,1)S(1)}, bf16[32,1536]{1,0:T(8,128)(2,1)}, u32[]{:S(2)}) copy-start(bf16[32,1536]{1,0:T(8,128)(2,1)} %get-tuple-element.27) | copy-start | bytes 294916
  67.3 3.6 %copy-start.2 = (bf16[32,1536]{1,0:T(8,128)(2,1)S(1)}, bf16[32,1536]{1,0:T(8,128)(2,1)}, u32[]{:S(2)}) copy-start(bf16[32,1536]{1,0:T(8,128)(2,1)} %get-tuple-element.28) | copy-start | bytes 294916
  67.3 4.2 %copy-start.1 = (bf16[32,1536]{1,0:T(8,128)(2,1)S(1)}, bf16[32,1536]{1,0:T(8,128)(2,1)}, u32[]{:S(2)}) copy-start(bf16[32,1536]{1,0:T(8,128)(2,1)} %get-tuple-element.29) | copy-start | bytes 294916
  67.3 4.8 %copy-start.6 = (bf16[64,384]{1,0:T(8,128)(2,1)S(1)}, bf16[64,384]{1,0:T(8,128)(2,1)}, u32[]{:S(2)}) copy-start(bf16[64,384]{1,0:T(8,128)(2,1)} %get-tuple-element.30) | copy-start | bytes 147460
  67.3 5.4 %copy-start.5 = (bf16[64,384]{1,0:T(8,128)(2,1)S(1)}, bf16[64,384]{1,0:T(8,128)(2,1)}, u32[]{:S(2)}) copy-start(bf16[64,384]{1,0:T(8,128)(2,1)} %get-tuple-element.31) | copy-start | bytes 147460
  67.3 6.1 %copy-start.4 = (bf16[64,384]{1,0:T(8,128)(2,1)S(1)}, bf16[64,384]{1,0:T(8,128)(2,1)}, u32[]{:S(2)}) copy-start(bf16[64,384]{1,0:T(8,128)(2,1)} %get-tuple-element.32) | copy-start | bytes 147460
  67.3 6.7 %copy-start = (f32[64,1536]{1,0:T(8,128)S(1)}, f32[64,1536]{1,0:T(8,128)}, u32[]{:S(2)}) copy-start(f32[64,1536]{1,0:T(8,128)} %get-tuple-element.34) | copy-start | bytes 1179652
  67.3 7.4 %copy-start.7 = (f32[8,12]{1,0:T(8,128)S(1)}, f32[8,12]{1,0:T(8,128)}, u32[]{:S(2)}) copy-start(f32[8,12]{1,0:T(8,128)} %get-tuple-element.35) | copy-start | bytes 1156

commit v3 on v2

--- a/solution.py
+++ b/solution.py
@@ -428,18 +428,21 @@
 
     pl.semaphore_wait(barrier, peers - 1 + planes)
 
-    def first_send(h):
-        return send(stage.at[h], recv.at[me], s1.at[h], r1.at[me], home(h))
-
-    def first_recv(p):
-        return send(stage.at[0], recv.at[p], s1.at[0], r1.at[p], partner)
-
-    for i in range(heads):
-        h = lax.rem(me + i, heads)
-
-        @pl.when(me != home_peer(h))
-        def _():
-            first_send(h).start()
+    def first_send(h, k):
+        at = pl.ds(k * 2 * rows, 2 * rows)
+        return send(stage.at[h, at], recv.at[me, at], s1.at[k, h], r1.at[k, me], home(h))
+
+    def first_recv(p, k):
+        at = pl.ds(k * 2 * rows, 2 * rows)
+        return send(stage.at[0, at], recv.at[p, at], s1.at[k, 0], r1.at[k, p], partner)
+
+    for k in range(2):
+        for i in range(heads):
+            h = lax.rem(me + i, heads)
+
+            @pl.when(me != home_peer(h))
+            def _():
+                first_send(h, k).start()
 
     def text_sources():
         cols = pl.ds(pl.multiple_of(lane_block * HEAD_SIZE, HEAD_SIZE), HEAD_SIZE)
@@ -476,11 +479,7 @@
     def column_send(t):
         return send(xst.at[t], xcol.at[s], s6.at[t], r6.at[s], (t, g))
 
-    for i in range(1, seq):
-        column_send(lax.rem(s + i, seq)).start()
-    xcol[pl.ds(s, 1)] = xst[pl.ds(s, 1)]
-
-    xlow = dot(x_ref[...], downw_ref[...])
+    xlow = dot(x_ref[...], downw_ref[...], NT)
     xlow_out[...] = jnp.concatenate([xlow[0:hrows], xlow[hrows:rows]], axis=1).astype(BF)
 
     def low_send(h):
@@ -500,6 +499,38 @@
         return send(
             up_out.at[c], up_all.at[mine, c], s9.at[p], r9.at[mine], peer(p)
         )
+
+    def column_sends():
+        for i in range(1, seq):
+            column_send(lax.rem(s + i, seq)).start()
+        xcol[pl.ds(s, 1)] = xst[pl.ds(s, 1)]
+
+    @pl.when(jnp.logical_not(is_head))
+    def _():
+        column_sends()
+
+    def up_trade():
+        return send(up_in2.at[0, 1 - c], up_in2.at[1, 0], s8.at[0], r8.at[0], partner)
+
+    def text_trade():
+        return send(to, ti, s3.at[2], r3.at[2], partner)
+
+    def back_query(p):
+        return send(
+            dqall.at[pl.ds(pl.multiple_of(p * rows, rows), rows)], ret.at[mine, pl.ds(0, rows)],
+            s4.at[0, p], r4.at[0, mine], peer(p)
+        )
+
+    def back_send(k, p):
+        at = pl.ds(k * rows, rows)
+        return send(ost.at[p, at], ret.at[mine, at], s4.at[k, p], r4.at[k, mine], peer(p))
+
+    def back_recv(k, h):
+        at = pl.ds(k * rows, rows)
+        return send(ost.at[0, at], ret.at[h, at], s4.at[k, 0], r4.at[k, h], partner)
+
+    def trade(k):
+        return send(xo.at[k], xi.at[k], s3.at[k], r3.at[k], partner)
 
     @pl.when(is_head)
     def _():
@@ -509,7 +540,7 @@
 
             @pl.when(me != p)
             def _():
-                first_recv(p).wait_recv()
+                first_recv(p, 0).wait_recv()
 
         swap = send(recv.at[:, pl.ds(0, 2 * rows)], kv2, s2.at[0], r2.at[0], partner)
         swap.start()
@@ -520,6 +551,13 @@
 
         kall[0:image] = recv[:, 0:rows].reshape(image, HEAD_SIZE)
         vall[0:image] = dequant(recv[:, rows : 2 * rows])
+        for p in range(peers):
+
+            @pl.when(me != p)
+            def _():
+                first_recv(p, 1).wait_recv()
+
+        column_sends()
         qall[0:image] = recv[:, 2 * rows : 3 * rows].reshape(image, HEAD_SIZE)
         doall[0:image] = recv[:, 3 * rows : 4 * rows].reshape(image, HEAD_SIZE)
 
@@ -547,8 +585,9 @@
         def query_block(index, carried):
             at = pl.ds(pl.multiple_of(index * half, half), half)
             queries, grads = qall[at], doall[at]
-            scores = dot(kall[...], queries, NT) * scale
-            expo = jnp.exp(scores - jnp.max(scores, axis=0, keepdims=True))
+            scores = dot(kall[...], queries, NT)
+            top = jnp.max(scores, axis=0, keepdims=True) * (scale * math.log2(math.e))
+            expo = jnp.exp2(scores * (scale * math.log2(math.e)) - top)
             probs = expo * (1.0 / jnp.sum(expo, axis=0, keepdims=True))
             dvacc[...] += dot(probs.astype(BF), grads)
             dprobs = dot(vall[...], grads, NT)
@@ -556,35 +595,46 @@
             dscores = (probs * (dprobs - deltas)).astype(BF)
             dkacc[...] += dot(dscores, queries)
             dqall[at] = (dot(ktr[...], dscores).T * scale).astype(BF)
+
+            @pl.when(index < image // half)
+            def _():
+                for i in range(half // rows):
+                    p = index * (half // rows) + i
+
+                    @pl.when(p != me)
+                    def _():
+                        back_query(p).start()
+
             return carried
 
         lax.fori_loop(0, (image + half) // half, query_block, 0)
+        xo[1] = dvacc[image : 2 * image].astype(BF)
+        trade(1).start()
         xo[0] = (dkacc[image : 2 * image] * scale).astype(BF)
-        xo[1] = dvacc[image : 2 * image].astype(BF)
-        trade = send(xo, xi, s3.at[0], r3.at[0], partner)
-        trade.start()
-        text_trade = send(to, ti, s3.at[1], r3.at[1], partner)
+        trade(0).start()
+        trade(1).wait_recv()
+        ost[:, 2 * rows : 3 * rows] = (
+            (dvacc[0:image] + xi[1].astype(F32)).astype(BF).reshape(peers, rows, HEAD_SIZE)
+        )
+        for i in range(1, peers):
+            back_send(2, lax.rem(me + i, peers)).start()
+        trade(0).wait_recv()
+        ost[:, rows : 2 * rows] = (
+            (dkacc[0:image] * scale + xi[0].astype(F32)).astype(BF).reshape(peers, rows, HEAD_SIZE)
+        )
+        for i in range(1, peers):
+            back_send(1, lax.rem(me + i, peers)).start()
+        ret[pl.ds(mine, 1), rows : 3 * rows] = ost[pl.ds(me, 1), rows : 3 * rows]
+        ret[pl.ds(mine, 1), 0:rows] = dqall[pl.ds(pl.multiple_of(me * rows, rows), rows)].reshape(
+            1, rows, HEAD_SIZE
+        )
 
         @pl.when(takes_text)
         def _():
             to[0:text] = (dkacc[2 * image : 2 * image + text] * scale).astype(BF)
             to[text : 2 * text] = dvacc[2 * image : 2 * image + text].astype(BF)
             to[2 * text : 2 * text + half] = dqall[image : image + half]
-            text_trade.start()
-
-        ost[:, 0:rows] = dqall[0:image].reshape(peers, rows, HEAD_SIZE)
-        trade.wait_recv()
-        ost[:, rows : 2 * rows] = (
-            (dkacc[0:image] * scale + xi[0].astype(F32)).astype(BF).reshape(peers, rows, HEAD_SIZE)
-        )
-        ost[:, 2 * rows : 3 * rows] = (
-            (dvacc[0:image] + xi[1].astype(F32)).astype(BF).reshape(peers, rows, HEAD_SIZE)
-        )
-        for i in range(1, peers):
-            p = lax.rem(me + i, peers)
-            send(ost.at[p], ret.at[mine], s4.at[p], r4.at[mine], peer(p)).start()
-
-        ret[pl.ds(mine, 1)] = ost[pl.ds(me, 1)]
+            text_trade().start()
 
         for p in range(peers):
 
@@ -599,14 +649,46 @@
         early = dot(low_rows, kept[:, 0:hrows].reshape(peers * hrows, HEAD_SIZE))
         late = dot(low_rows, kept[:, hrows:rows].reshape(peers * hrows, HEAD_SIZE))
         part_up = (early[0:rank] + late[rank : 2 * rank]).reshape(2, hrank, HEAD_SIZE)
-        up_out32 = up_in2.at[0]
-        up_out32[...] = part_up
-        up_trade = send(up_in2.at[0, 1 - c], up_in2.at[1, 0], s8.at[0], r8.at[0], partner)
-        up_trade.start()
-
+        up_in2[0] = part_up
+        up_trade().start()
+
+    low = jnp.zeros((rows, rank), F32)
+    sums = []
+    for h in range(heads):
+
+        @pl.when(me != home_peer(h))
+        def _():
+            back_recv(2, h).wait_recv()
+
+        cols = slice(h * HEAD_SIZE, (h + 1) * HEAD_SIZE)
+        codes = code_ref[:, cols]
+        inside = jnp.abs(codes) < QMAX
+        value_grad = ret[h, 2 * rows : 3 * rows].astype(F32)
+        kept = jnp.where(inside, value_grad, 0.0).astype(BF)
+        lsq_term = jnp.where(inside, -frac_ref[:, cols].astype(F32), codes.astype(F32))
+        sums.append(jnp.sum(value_grad * lsq_term, axis=0, keepdims=True))
+        low = low + dot(kept, upw_ref[:, cols], NT)
+        dv_ref[:, cols] = kept
+
+    sums.append(jnp.zeros((rows - heads, HEAD_SIZE), F32))
+    step_terms = jnp.sum(jnp.concatenate(sums, axis=0), axis=1, keepdims=True)
+    step_high = step_terms.astype(BF).astype(F32)
+    lane_at = lax.broadcasted_iota(jnp.int32, (rows, rank), 1)
+    beside = jnp.where(lane_at == 0, step_high, jnp.where(lane_at == 1, step_terms - step_high, 0.0))
+    low_out[...] = jnp.concatenate([low, beside], axis=1).astype(BF)
+
+    def tile_send(t):
+        return send(low_out, low_in.at[s], s10.at[t], r10.at[s], (t, g))
+
+    for i in range(1, seq):
+        tile_send(lax.rem(s + i, seq)).start()
+    low_in[pl.ds(s, 1)] = low_out[...].reshape(1, rows, HEAD_SIZE)
+
+    @pl.when(is_head)
+    def _():
         @pl.when(holds_text)
         def _():
-            text_trade.wait_recv()
+            text_trade().wait_recv()
             full = (seq, share, HEAD_SIZE)
             tfin[0 : seq // 2, 0] = dqall[image : image + half].reshape(seq // 2, share, HEAD_SIZE)
             tfin[seq // 2 : seq, 0] = ti[2 * text : 2 * text + half].reshape(seq // 2, share, HEAD_SIZE)
@@ -624,7 +706,7 @@
 
             rett[pl.ds(lane_block, 1)] = tfin[pl.ds(s, 1)]
 
-        up_trade.wait_recv()
+        up_trade().wait_recv()
         up_out[pl.ds(c, 1)] = (
             (up_in2[pl.ds(0, 1), pl.ds(c, 1)] + up_in2[pl.ds(1, 1), pl.ds(0, 1)]) * unscale
         ).astype(BF).reshape(1, hrank, HEAD_SIZE)
@@ -632,42 +714,50 @@
             up_send(lax.rem(me + i, peers)).start()
         up_all[pl.ds(mine, 1), pl.ds(c, 1)] = up_out[pl.ds(c, 1)].reshape(1, 1, hrank, HEAD_SIZE)
 
-    low = jnp.zeros((rows, rank), F32)
-    lane = lax.broadcasted_iota(jnp.int32, (1, HEAD_SIZE), 1)
-    step_terms = jnp.zeros((1, HEAD_SIZE), F32)
-    for h in range(heads):
-
-        @pl.when(me != home_peer(h))
-        def _():
-            send(ost.at[0], ret.at[h], s4.at[0], r4.at[h], partner).wait_recv()
-
-        cols = slice(h * HEAD_SIZE, (h + 1) * HEAD_SIZE)
-        codes = code_ref[:, cols]
-        inside = jnp.abs(codes) < QMAX
-        value_grad = ret[h, 2 * rows : 3 * rows].astype(F32)
-        kept = jnp.where(inside, value_grad, 0.0).astype(BF)
-        lsq_term = jnp.where(inside, -frac_ref[:, cols].astype(F32), codes.astype(F32))
-        total = jnp.sum(value_grad * lsq_term)
-        step_terms = step_terms + jnp.where(lane == h, total, 0.0)
-        low = low + dot(kept, upw_ref[:, cols], NT)
-        dq_ref[:, cols] = ret[h, 0:rows]
-        dk_ref[:, cols] = ret[h, rows : 2 * rows]
-        dv_ref[:, cols] = kept
-
-    step_high = step_terms.astype(BF).astype(F32)
-    step_low = step_terms - step_high
-    row_at = lax.broadcasted_iota(jnp.int32, (rows, rank), 0)
-    beside = jnp.where(
-        row_at == 0, step_high[:, 0:rank], jnp.where(row_at == 1, step_low[:, 0:rank], 0.0)
-    )
-    low_out[...] = jnp.concatenate([low, beside], axis=1).astype(BF)
-
-    def tile_send(t):
-        return send(low_out, low_in.at[s], s10.at[t], r10.at[s], (t, g))
-
-    for i in range(1, seq):
-        tile_send(lax.rem(s + i, seq)).start()
-    low_in[pl.ds(s, 1)] = low_out[...].reshape(1, rows, HEAD_SIZE)
+    for t in range(seq):
+
+        @pl.when(s != t)
+        def _():
+            send(xst.at[0], xcol.at[t], s6.at[0], r6.at[t], partner).wait_recv()
+            send(low_out, low_in.at[t], s10.at[0], r10.at[t], partner).wait_recv()
+
+    tiles = low_in[...]
+    flat = tiles.reshape(seq * rows, HEAD_SIZE).T
+    block = dot(flat, xcol[...].reshape(seq * rows, wide))[0:rank]
+    step_group = jnp.sum(tiles[:, 0:16].astype(F32), axis=0)
+    for other in range(head):
+        red_out[other, 0:part] = block[other * part : (other + 1) * part]
+        red_out[other, part : part + 16, 0:HEAD_SIZE] = step_group
+        red_out[other, part : part + 16, HEAD_SIZE:wide] = jnp.zeros((16, wide - HEAD_SIZE), F32)
+
+    def reduce_send(other):
+        return send(red_out.at[other], red_in.at[g], s11.at[other], r11.at[g], (s, other))
+
+    for i in range(1, head):
+        reduce_send(lax.rem(g + i, head)).start()
+    red_in[pl.ds(g, 1)] = red_out[pl.ds(g, 1)]
+    for other in range(head):
+
+        @pl.when(g != other)
+        def _():
+            send(red_out.at[0], red_in.at[other], s11.at[0], r11.at[other], partner).wait_recv()
+
+    summed = jnp.sum(red_in[...], axis=0)
+    gath[pl.ds(y, 1), pl.ds(c, 1), pl.ds(s, 1)] = (
+        (summed[0:part] * unscale).astype(BF).reshape(1, 1, 1, part, wide)
+    )
+
+    def row_send(p):
+        return send(gath.at[y, c, s], gath.at[y, c, s], s12.at[p], r12.at[me], peer(p))
+
+    def core_send():
+        return send(gath.at[:, c], gath.at[:, c], s12.at[peers], r12.at[peers], partner)
+
+    def core_up_send():
+        return send(up_all.at[:, c], up_all.at[:, c], s8.at[1], r8.at[1], partner)
+
+    for i in range(1, peers):
+        row_send(lax.rem(me + i, peers)).start()
 
     for j in range(group):
 
@@ -680,63 +770,25 @@
         dkt_ref[:, cols] = rett[j, 1]
         dvt_ref[:, cols] = rett[j, 2]
 
-    for t in range(seq):
-
-        @pl.when(s != t)
-        def _():
-            send(xst.at[0], xcol.at[t], s6.at[0], r6.at[t], partner).wait_recv()
-            send(low_out, low_in.at[t], s10.at[0], r10.at[t], partner).wait_recv()
-
-    tiles = low_in[...]
-    flat = tiles.reshape(seq * rows, HEAD_SIZE).T
-    block = dot(flat, xcol[...].reshape(seq * rows, wide))[0:rank]
-    step_group = jnp.sum(
-        jnp.sum(tiles[:, 0:2].astype(F32), axis=0), axis=0, keepdims=True
-    )
-    for other in range(head):
-        red_out[other, 0:part] = block[other * part : (other + 1) * part]
-        red_out[other, part : part + 8, 0:HEAD_SIZE] = jnp.broadcast_to(step_group, (8, HEAD_SIZE))
-        red_out[other, part : part + 8, HEAD_SIZE:wide] = jnp.zeros((8, wide - HEAD_SIZE), F32)
-
-    def reduce_send(other):
-        return send(red_out.at[other], red_in.at[g], s11.at[other], r11.at[g], (s, other))
-
-    for i in range(1, head):
-        reduce_send(lax.rem(g + i, head)).start()
-    red_in[pl.ds(g, 1)] = red_out[pl.ds(g, 1)]
-    for other in range(head):
-
-        @pl.when(g != other)
-        def _():
-            send(red_out.at[0], red_in.at[other], s11.at[0], r11.at[other], partner).wait_recv()
-
-    summed = jnp.sum(red_in[...], axis=0)
-    gath[pl.ds(y, 1), pl.ds(c, 1), pl.ds(s, 1)] = (
-        (summed[0:part] * unscale).astype(BF).reshape(1, 1, 1, part, wide)
-    )
-
-    def row_send(t):
-        return send(
-            gath.at[y, c, s], gath.at[y, c, s], s12.at[t], r12.at[s], (t, g)
-        )
-
-    def plane_send(i):
-        to_plane = lax.rem(y + i, planes)
-        return send(
-            gath.at[y, c], gath.at[y, c], s12.at[seq + i], r12.at[seq + y], (s, to_plane * 2 + c)
-        )
-
-    def core_send():
-        return send(gath.at[:, c], gath.at[:, c], s12.at[seq], r12.at[seq + planes], partner)
-
-    def core_up_send():
-        return send(up_all.at[:, c], up_all.at[:, c], s8.at[1], r8.at[1], partner)
-
-    for i in range(1, seq):
-        row_send(lax.rem(s + i, seq)).start()
+    for h in range(heads):
+
+        @pl.when(me != home_peer(h))
+        def _():
+            back_recv(0, h).wait_recv()
+            back_recv(1, h).wait_recv()
+
+        cols = slice(h * HEAD_SIZE, (h + 1) * HEAD_SIZE)
+        dq_ref[:, cols] = ret[h, 0:rows]
+        dk_ref[:, cols] = ret[h, rows : 2 * rows]
 
     slot_index = group_ref[time_ref[0]]
-    step_row = summed[part : part + 1, HEAD_SIZE // 2 : HEAD_SIZE // 2 + heads] * (QMAX ** (-0.5) * unscale)
+    lanes = summed[part : part + 16, 0:HEAD_SIZE]
+    lane_at = lax.broadcasted_iota(jnp.int32, (16, HEAD_SIZE), 1)
+    row_at = lax.broadcasted_iota(jnp.int32, (16, HEAD_SIZE), 0)
+    chosen = jnp.logical_or(lane_at == rank, lane_at == rank + 1)
+    head_sums = jnp.sum(jnp.where(chosen, lanes, 0.0), axis=1, keepdims=True)
+    step_row = jnp.sum(jnp.where(lane_at == row_at, head_sums, 0.0), axis=0, keepdims=True)[:, 0:heads]
+    step_row = step_row * (QMAX ** (-0.5) * unscale)
     slots = steps_ref.shape[0]
     slot_at = lax.broadcasted_iota(jnp.int32, (slots, heads), 0)
     steps_ref[...] = jnp.where(slot_at == slot_index, jnp.broadcast_to(step_row, (slots, heads)), 0.0)
@@ -749,60 +801,57 @@
 
     core_up_send().start()
 
-    for t in range(seq):
-
-        @pl.when(s != t)
-        def _():
-            send(gath.at[y, c, t], gath.at[y, c, t], s12.at[0], r12.at[t], partner).wait_recv()
-
-    for i in range(1, planes):
-        plane_send(i).start()
-    for i in range(1, planes):
-        from_plane = lax.rem(y + i, planes)
-        send(
-            gath.at[from_plane, c], gath.at[from_plane, c], s12.at[seq + i], r12.at[seq + from_plane], partner
-        ).wait_recv()
+    for p in range(peers):
+
+        @pl.when(me != p)
+        def _():
+            block_at = gath.at[p % planes, c, p // planes]
+            send(block_at, block_at, s12.at[0], r12.at[p], partner).wait_recv()
+
     core_send().start()
     send(up_all.at[:, 1 - c], up_all.at[:, 1 - c], s8.at[1], r8.at[1], partner).wait_recv()
     for h in range(heads):
         cols = slice(h * HEAD_SIZE, (h + 1) * HEAD_SIZE)
         up_ref[:, cols] = up_all[h].reshape(rank, HEAD_SIZE).astype(F32)
-    send(gath.at[:, 1 - c], gath.at[:, 1 - c], s12.at[seq], r12.at[seq + planes], partner).wait_recv()
+    send(gath.at[:, 1 - c], gath.at[:, 1 - c], s12.at[peers], r12.at[peers], partner).wait_recv()
     for t in range(seq):
-        down_ref[t * wide : (t + 1) * wide] = gath[:, :, t].reshape(rank, wide).astype(F32).T
+        down_ref[:, t * wide : (t + 1) * wide] = gath[:, :, t].reshape(rank, wide).astype(F32)
 
     for h in range(heads):
 
         @pl.when(me != home_peer(h))
         def _():
-            first_send(h).wait_send()
+            first_send(h, 0).wait_send()
+            first_send(h, 1).wait_send()
             low_send(h).wait_send()
 
     for i in range(1, seq):
         t = lax.rem(s + i, seq)
         column_send(t).wait_send()
         tile_send(t).wait_send()
-        row_send(t).wait_send()
     for i in range(1, head):
         reduce_send(lax.rem(g + i, head)).wait_send()
-    for i in range(1, planes):
-        plane_send(i).wait_send()
+    for i in range(1, peers):
+        row_send(lax.rem(me + i, peers)).wait_send()
     core_send().wait_send()
     core_up_send().wait_send()
 
     @pl.when(is_head)
     def _():
         send(recv.at[:, pl.ds(0, 2 * rows)], kv2, s2.at[0], r2.at[0], partner).wait_send()
-        send(xo, xi, s3.at[0], r3.at[0], partner).wait_send()
-        send(up_in2.at[0, 1 - c], up_in2.at[1, 0], s8.at[0], r8.at[0], partner).wait_send()
+        trade(0).wait_send()
+        trade(1).wait_send()
+        up_trade().wait_send()
         for i in range(1, peers):
             p = lax.rem(me + i, peers)
-            send(ost.at[p], ret.at[mine], s4.at[p], r4.at[mine], peer(p)).wait_send()
+            back_query(p).wait_send()
+            back_send(1, p).wait_send()
+            back_send(2, p).wait_send()
             up_send(p).wait_send()
 
     @pl.when(takes_text)
     def _():
-        send(to, ti, s3.at[1], r3.at[1], partner).wait_send()
+        text_trade().wait_send()
 
     @pl.when(holds_text)
     def _():
@@ -813,6 +862,31 @@
             send(
                 tfin.at[other], rett.at[lane_block], s5.at[other], r5.at[lane_block], (other, g)
             ).wait_send()
+
+
+def settle_kernel(count, *refs):
+    sources, targets, done = refs[:count], refs[count : 2 * count], refs[2 * count]
+    copies = [
+        pltpu.make_async_copy(source, target, done.at[i])
+        for i, (source, target) in enumerate(zip(sources, targets))
+    ]
+    for copy in copies:
+        copy.start()
+    for copy in copies:
+        copy.wait()
+
+
+def settle(arrays):
+    count = len(arrays)
+    anywhere = pl.BlockSpec(memory_space=pl.ANY)
+    return pl.pallas_call(
+        functools.partial(settle_kernel, count),
+        out_shape=[jax.ShapeDtypeStruct(a.shape, a.dtype) for a in arrays],
+        in_specs=[anywhere] * count,
+        out_specs=[anywhere] * count,
+        scratch_shapes=[pltpu.SemaphoreType.DMA((count,))],
+        name="settle",
+    )(*arrays)
 
 
 def whole_heads(
@@ -846,12 +920,12 @@
     sems = pltpu.SemaphoreType.DMA
     hbm = pl.BlockSpec(memory_space=pl.ANY)
     smem = pl.BlockSpec(memory_space=pltpu.SMEM)
-    return tuple(pl.pallas_call(
+    results = pl.pallas_call(
         functools.partial(attention_kernel, seq, head),
         out_shape=[jax.ShapeDtypeStruct((rows, width), BF)] * 3
         + [jax.ShapeDtypeStruct((share, text_width), BF)] * 3
         + [
-            jax.ShapeDtypeStruct(adapter_down_weight.shape, F32),
+            jax.ShapeDtypeStruct(adapter_down_weight.shape[::-1], F32),
             jax.ShapeDtypeStruct(adapter_up_weight.shape, F32),
             jax.ShapeDtypeStruct(value_step_sizes.shape, F32),
         ],
@@ -865,7 +939,7 @@
             pltpu.VMEM(image_input_rows.shape, BF),
             pltpu.VMEM((rows, width), BF),
             pltpu.VMEM(adapter_up_weight.shape, BF),
-            pltpu.VMEM(adapter_down_weight.shape, BF),
+            pltpu.VMEM(adapter_down_weight.shape[::-1], BF),
             pltpu.VMEM((heads, 4 * rows, HEAD_SIZE), BF),
             pltpu.VMEM((peers, 4 * rows, HEAD_SIZE), BF),
             pltpu.VMEM((peers, 2 * rows, HEAD_SIZE), BF),
@@ -896,20 +970,20 @@
             pltpu.VMEM((heads, 2, rank // 2, HEAD_SIZE), BF),
             pltpu.VMEM((rows, HEAD_SIZE), BF),
             pltpu.VMEM((seq, rows, HEAD_SIZE), BF),
-            pltpu.VMEM((head, rank // head + 8, wide), F32),
-            pltpu.VMEM((head, rank // head + 8, wide), F32),
+            pltpu.VMEM((head, rank // head + 16, wide), F32),
+            pltpu.VMEM((head, rank // head + 16, wide), F32),
             pltpu.VMEM((planes, 2, seq, rank // head, wide), BF),
             sems((12,)),
-            sems((heads,)),
-            sems((peers,)),
+            sems((2, heads)),
+            sems((2, peers)),
             sems((1,)),
             sems((1,)),
             sems((4,)),
             sems((4,)),
-            sems((2,)),
-            sems((2,)),
-            sems((peers,)),
-            sems((heads,)),
+            sems((3,)),
+            sems((3,)),
+            sems((3, peers)),
+            sems((3, heads)),
             sems((seq,)),
             sems((group,)),
             sems((seq,)),
@@ -924,8 +998,8 @@
             sems((seq,)),
             sems((head,)),
             sems((head,)),
-            sems((seq + planes,)),
-            sems((seq + planes + 1,)),
+            sems((peers + 1,)),
+            sems((peers + 1,)),
         ],
         compiler_params=pltpu.CompilerParams(
             collective_id=0, has_side_effects=True, vmem_limit_bytes=56 * 1024 * 1024
@@ -943,11 +1017,13 @@
         image_input_rows,
         value_fraction,
         adapter_up_weight,
-        adapter_down_weight,
+        adapter_down_weight.T,
         value_step_sizes,
         timestep_group,
         timestep,
-    ))
+    )
+    results = settle(results)
+    return (*results[:6], results[6].T, *results[7:])
 
 
 def pick(mesh):
@@ -963,7 +1039,9 @@
             and seq >= pair
             and rows % 32 == 0
             and 2 * arguments[2].shape[0] == HEAD_SIZE
-            and width // HEAD_SIZE <= arguments[2].shape[0]
+            and width // HEAD_SIZE <= 16
+            and (text // 2) % rows == 0
+            and (seq * head // 2 * rows) % (text // 2) == 0
             and arguments[2].shape[0] % (16 * head) == 0
             and arguments[0].shape[1] % (seq * HEAD_SIZE) == 0
             and text % (seq * 16) == 0

time: 76.1 us -> 104 us (1.37)
  Pallas kernels: 63.8 us -> 103 us
  local copies, waits for them, and re-layouts: 10.2 us -> 0 us
    pallas_call x0 -> x1, Pallas kernels: none -> 50.5 us  [settle(): pl.pallas_call(functools.partial(settle_kernel, count), out_shape=[jax.Sh...]
    pallas_call x1, Pallas kernels: 63.8 us -> 52.1 us  [whole_heads(): pl.pallas_call(functools.partial(attention_kernel, seq, head), out_shape=...]
    unnamed x25 -> x0, local copies, waits for them, and re-layouts: 7.31 us -> none
    pallas_call x1 -> x0, local copies, waits for them, and re-layouts: 2.85 us -> none  [whole_heads(): pl.pallas_call(functools.partial(attention_kernel, seq, head), out_shape=...]
where the time goes in v3:
time: 104 us
  Pallas kernels  103 us (99%)
  between operations  1.3 us (1%)
    pallas_call x1, Pallas kernels, whole_heads(): pl.pallas_call(functools.partial(attention_kernel, seq, head), out_shape=...  52.1 us
    pallas_call x1, Pallas kernels, settle(): pl.pallas_call(functools.partial(settle_kernel, count), out_shape=[jax.Sh...  50.5 us

profile of v3, /device:TPU:0, one launch (start us, length us, event | category | flops | bytes accessed | tf_op | source)
XLA Modules:
  0.0 103.9 jit_solution(928985273594936197)
XLA Ops:
  1.3 52.1 %whole_heads.1 = (bf16[32,1536]{1,0:T(8,128)(2,1)}, bf16[32,1536]{1,0:T(8,128)(2,1)}, bf16[32,1536]{1,0:T(8,128)(2,1)}, bf16[64,384]{1,0:T(8,128)(2,1)}, bf16[64...) custom-call(bf16[32,1536]{1,0:T(8,128)(2,1)} %q_in.1, ...), custom_call_target="tpu_custom_call" | custom-call | tf_op jit(solution)/shard_map/whole_heads/pallas_call | solution.py:923
  53.4 50.5 %settle.1 = (bf16[32,1536]{1,0:T(8,128)(2,1)}, bf16[32,1536]{1,0:T(8,128)(2,1)}, bf16[32,1536]{1,0:T(8,128)(2,1)}, bf16[64,384]{1,0:T(8,128)(2,1)}, bf16[64,384]...) custom-call(bf16[32,1536]{1,0:T(8,128)(2,1)} %get-tuple-element.27.refs, ...), custom_call_target="tpu_custom_call" | custom-call | tf_op jit(solution)/shard_map/settle/pallas_call | solution.py:882

commit v4 on v3

--- a/solution.py
+++ b/solution.py
@@ -315,6 +315,8 @@
     low_in,
     red_out,
     red_in,
+    sum_out,
+    sum_in,
     gath,
     li,
     s1,
@@ -536,11 +538,9 @@
     def _():
         recv[pl.ds(me, 1)] = stage[pl.ds(mine, 1)]
         xlow_in[pl.ds(me, 1)] = xlow_out[...].reshape(1, hrows, HEAD_SIZE)
-        for p in range(peers):
-
-            @pl.when(me != p)
-            def _():
-                first_recv(p, 0).wait_recv()
+        for i in range(1, peers):
+            p = lax.rem(me + i, peers)
+            first_recv(p, 0).wait_recv()
 
         swap = send(recv.at[:, pl.ds(0, 2 * rows)], kv2, s2.at[0], r2.at[0], partner)
         swap.start()
@@ -551,11 +551,9 @@
 
         kall[0:image] = recv[:, 0:rows].reshape(image, HEAD_SIZE)
         vall[0:image] = dequant(recv[:, rows : 2 * rows])
-        for p in range(peers):
-
-            @pl.when(me != p)
-            def _():
-                first_recv(p, 1).wait_recv()
+        for i in range(1, peers):
+            p = lax.rem(me + i, peers)
+            first_recv(p, 1).wait_recv()
 
         column_sends()
         qall[0:image] = recv[:, 2 * rows : 3 * rows].reshape(image, HEAD_SIZE)
@@ -579,35 +577,28 @@
         kall[image : 2 * image] = kv2[:, 0:rows].reshape(image, HEAD_SIZE)
         vall[image : 2 * image] = dequant(kv2[:, rows : 2 * rows])
         ktr[...] = kall[...].T
-        dkacc[...] = jnp.zeros_like(dkacc)
-        dvacc[...] = jnp.zeros_like(dvacc)
-
-        def query_block(index, carried):
-            at = pl.ds(pl.multiple_of(index * half, half), half)
+
+        def query_block(index):
+            at = slice(index * half, (index + 1) * half)
             queries, grads = qall[at], doall[at]
             scores = dot(kall[...], queries, NT)
+            dprobs = dot(vall[...], grads, NT)
             top = jnp.max(scores, axis=0, keepdims=True) * (scale * math.log2(math.e))
             expo = jnp.exp2(scores * (scale * math.log2(math.e)) - top)
             probs = expo * (1.0 / jnp.sum(expo, axis=0, keepdims=True))
-            dvacc[...] += dot(probs.astype(BF), grads)
-            dprobs = dot(vall[...], grads, NT)
+            value_part = dot(probs.astype(BF), grads)
             deltas = jnp.sum(probs * dprobs, axis=0, keepdims=True)
             dscores = (probs * (dprobs - deltas)).astype(BF)
-            dkacc[...] += dot(dscores, queries)
+            key_part = dot(dscores, queries)
+            dvacc[...] = value_part if index == 0 else dvacc[...] + value_part
+            dkacc[...] = key_part if index == 0 else dkacc[...] + key_part
             dqall[at] = (dot(ktr[...], dscores).T * scale).astype(BF)
 
-            @pl.when(index < image // half)
-            def _():
-                for i in range(half // rows):
-                    p = index * (half // rows) + i
-
-                    @pl.when(p != me)
-                    def _():
-                        back_query(p).start()
-
-            return carried
-
-        lax.fori_loop(0, (image + half) // half, query_block, 0)
+        for index in range(image // half):
+            query_block(index)
+        for i in range(1, peers):
+            back_query(lax.rem(me + i, peers)).start()
+        query_block(image // half)
         xo[1] = dvacc[image : 2 * image].astype(BF)
         trade(1).start()
         xo[0] = (dkacc[image : 2 * image] * scale).astype(BF)
@@ -636,11 +627,9 @@
             to[2 * text : 2 * text + half] = dqall[image : image + half]
             text_trade().start()
 
-        for p in range(peers):
-
-            @pl.when(me != p)
-            def _():
-                send(xlow_out, xlow_in.at[p], s7.at[0], r7.at[p], partner).wait_recv()
+        for i in range(1, peers):
+            p = lax.rem(me + i, peers)
+            send(xlow_out, xlow_in.at[p], s7.at[0], r7.at[p], partner).wait_recv()
 
         codes = recv[:, rows : 2 * rows]
         kept = jnp.where(jnp.abs(codes.astype(F32)) < QMAX, ost[:, 2 * rows : 3 * rows].astype(F32), 0.0)
@@ -652,14 +641,14 @@
         up_in2[0] = part_up
         up_trade().start()
 
-    low = jnp.zeros((rows, rank), F32)
-    sums = []
     for h in range(heads):
 
         @pl.when(me != home_peer(h))
         def _():
             back_recv(2, h).wait_recv()
 
+    sums = []
+    for h in range(heads):
         cols = slice(h * HEAD_SIZE, (h + 1) * HEAD_SIZE)
         codes = code_ref[:, cols]
         inside = jnp.abs(codes) < QMAX
@@ -667,9 +656,9 @@
         kept = jnp.where(inside, value_grad, 0.0).astype(BF)
         lsq_term = jnp.where(inside, -frac_ref[:, cols].astype(F32), codes.astype(F32))
         sums.append(jnp.sum(value_grad * lsq_term, axis=0, keepdims=True))
-        low = low + dot(kept, upw_ref[:, cols], NT)
         dv_ref[:, cols] = kept
 
+    low = dot(dv_ref[...], upw_ref[...], NT)
     sums.append(jnp.zeros((rows - heads, HEAD_SIZE), F32))
     step_terms = jnp.sum(jnp.concatenate(sums, axis=0), axis=1, keepdims=True)
     step_high = step_terms.astype(BF).astype(F32)
@@ -714,38 +703,36 @@
             up_send(lax.rem(me + i, peers)).start()
         up_all[pl.ds(mine, 1), pl.ds(c, 1)] = up_out[pl.ds(c, 1)].reshape(1, 1, hrank, HEAD_SIZE)
 
-    for t in range(seq):
-
-        @pl.when(s != t)
-        def _():
-            send(xst.at[0], xcol.at[t], s6.at[0], r6.at[t], partner).wait_recv()
-            send(low_out, low_in.at[t], s10.at[0], r10.at[t], partner).wait_recv()
+    for i in range(1, seq):
+        t = lax.rem(s + i, seq)
+        send(xst.at[0], xcol.at[t], s6.at[0], r6.at[t], partner).wait_recv()
+        send(low_out, low_in.at[t], s10.at[0], r10.at[t], partner).wait_recv()
 
     tiles = low_in[...]
     flat = tiles.reshape(seq * rows, HEAD_SIZE).T
     block = dot(flat, xcol[...].reshape(seq * rows, wide))[0:rank]
     step_group = jnp.sum(tiles[:, 0:16].astype(F32), axis=0)
-    for other in range(head):
-        red_out[other, 0:part] = block[other * part : (other + 1) * part]
-        red_out[other, part : part + 16, 0:HEAD_SIZE] = step_group
-        red_out[other, part : part + 16, HEAD_SIZE:wide] = jnp.zeros((16, wide - HEAD_SIZE), F32)
+    red_out[...] = block.astype(BF).reshape(head, part, wide)
+    sum_out[...] = step_group
 
     def reduce_send(other):
-        return send(red_out.at[other], red_in.at[g], s11.at[other], r11.at[g], (s, other))
+        return send(red_out.at[other], red_in.at[g], s11.at[0, other], r11.at[0, g], (s, other))
+
+    def sum_send(other):
+        return send(sum_out, sum_in.at[g], s11.at[1, other], r11.at[1, g], (s, other))
 
     for i in range(1, head):
         reduce_send(lax.rem(g + i, head)).start()
+    for i in range(1, head):
+        sum_send(lax.rem(g + i, head)).start()
     red_in[pl.ds(g, 1)] = red_out[pl.ds(g, 1)]
-    for other in range(head):
-
-        @pl.when(g != other)
-        def _():
-            send(red_out.at[0], red_in.at[other], s11.at[0], r11.at[other], partner).wait_recv()
-
-    summed = jnp.sum(red_in[...], axis=0)
-    gath[pl.ds(y, 1), pl.ds(c, 1), pl.ds(s, 1)] = (
-        (summed[0:part] * unscale).astype(BF).reshape(1, 1, 1, part, wide)
-    )
+    sum_in[pl.ds(g, 1)] = step_group.reshape(1, 16, HEAD_SIZE)
+    for i in range(1, head):
+        other = lax.rem(g + i, head)
+        send(red_out.at[0], red_in.at[other], s11.at[0, 0], r11.at[0, other], partner).wait_recv()
+
+    summed = jnp.sum(red_in[...].astype(F32), axis=0) * unscale
+    gath[pl.ds(y, 1), pl.ds(c, 1), pl.ds(s, 1)] = summed.astype(BF).reshape(1, 1, 1, part, wide)
 
     def row_send(p):
         return send(gath.at[y, c, s], gath.at[y, c, s], s12.at[p], r12.at[me], peer(p))
@@ -777,12 +764,17 @@
             back_recv(0, h).wait_recv()
             back_recv(1, h).wait_recv()
 
+    for h in range(heads):
         cols = slice(h * HEAD_SIZE, (h + 1) * HEAD_SIZE)
         dq_ref[:, cols] = ret[h, 0:rows]
         dk_ref[:, cols] = ret[h, rows : 2 * rows]
 
     slot_index = group_ref[time_ref[0]]
-    lanes = summed[part : part + 16, 0:HEAD_SIZE]
+    for i in range(1, head):
+        other = lax.rem(g + i, head)
+        send(sum_out, sum_in.at[other], s11.at[1, 0], r11.at[1, other], partner).wait_recv()
+
+    lanes = jnp.sum(sum_in[...], axis=0)
     lane_at = lax.broadcasted_iota(jnp.int32, (16, HEAD_SIZE), 1)
     row_at = lax.broadcasted_iota(jnp.int32, (16, HEAD_SIZE), 0)
     chosen = jnp.logical_or(lane_at == rank, lane_at == rank + 1)
@@ -801,12 +793,10 @@
 
     core_up_send().start()
 
-    for p in range(peers):
-
-        @pl.when(me != p)
-        def _():
-            block_at = gath.at[p % planes, c, p // planes]
-            send(block_at, block_at, s12.at[0], r12.at[p], partner).wait_recv()
+    for i in range(1, peers):
+        p = lax.rem(me + i, peers)
+        block_at = gath.at[lax.rem(p, planes), c, p // planes]
+        send(block_at, block_at, s12.at[0], r12.at[p], partner).wait_recv()
 
     core_send().start()
     send(up_all.at[:, 1 - c], up_all.at[:, 1 - c], s8.at[1], r8.at[1], partner).wait_recv()
@@ -831,6 +821,7 @@
         tile_send(t).wait_send()
     for i in range(1, head):
         reduce_send(lax.rem(g + i, head)).wait_send()
+        sum_send(lax.rem(g + i, head)).wait_send()
     for i in range(1, peers):
         row_send(lax.rem(me + i, peers)).wait_send()
     core_send().wait_send()
@@ -865,15 +856,17 @@
 
 
 def settle_kernel(count, *refs):
-    sources, targets, done = refs[:count], refs[count : 2 * count], refs[2 * count]
-    copies = [
-        pltpu.make_async_copy(source, target, done.at[i])
-        for i, (source, target) in enumerate(zip(sources, targets))
-    ]
-    for copy in copies:
-        copy.start()
-    for copy in copies:
-        copy.wait()
+    sources, targets, held = refs[:count], refs[count : 2 * count], refs[2 * count : 3 * count]
+    came, went = refs[3 * count :]
+    loads = [pltpu.make_async_copy(a, b, came.at[i]) for i, (a, b) in enumerate(zip(sources, held))]
+    stores = [pltpu.make_async_copy(a, b, went.at[i]) for i, (a, b) in enumerate(zip(held, targets))]
+    for load in loads:
+        load.start()
+    for load, store in zip(loads, stores):
+        load.wait()
+        store.start()
+    for store in stores:
+        store.wait()
 
 
 def settle(arrays):
@@ -884,7 +877,9 @@
         out_shape=[jax.ShapeDtypeStruct(a.shape, a.dtype) for a in arrays],
         in_specs=[anywhere] * count,
         out_specs=[anywhere] * count,
-        scratch_shapes=[pltpu.SemaphoreType.DMA((count,))],
+        scratch_shapes=[pltpu.VMEM(a.shape, a.dtype) for a in arrays]
+        + [pltpu.SemaphoreType.DMA((count,))] * 2,
+        compiler_params=pltpu.CompilerParams(vmem_limit_bytes=56 * 1024 * 1024),
         name="settle",
     )(*arrays)
 
@@ -970,8 +965,10 @@
             pltpu.VMEM((heads, 2, rank // 2, HEAD_SIZE), BF),
             pltpu.VMEM((rows, HEAD_SIZE), BF),
             pltpu.VMEM((seq, rows, HEAD_SIZE), BF),
-            pltpu.VMEM((head, rank // head + 16, wide), F32),
-            pltpu.VMEM((head, rank // head + 16, wide), F32),
+            pltpu.VMEM((head, rank // head, wide), BF),
+            pltpu.VMEM((head, rank // head, wide), BF),
+            pltpu.VMEM((16, HEAD_SIZE), F32),
+            pltpu.VMEM((head, 16, HEAD_SIZE), F32),
             pltpu.VMEM((planes, 2, seq, rank // head, wide), BF),
             sems((12,)),
             sems((2, heads)),
@@ -996,8 +993,8 @@
             sems((heads,)),
             sems((seq,)),
             sems((seq,)),
-            sems((head,)),
-            sems((head,)),
+            sems((2, head)),
+            sems((2, head)),
             sems((peers + 1,)),
             sems((peers + 1,)),
         ],

time: 104 us -> 55.2 us (0.53)
  Pallas kernels: 103 us -> 53 us
    pallas_call x1, Pallas kernels: 50.5 us -> 2.53 us  [settle(): pl.pallas_call(functools.partial(settle_kernel, count), out_shape=[jax.Sh...]
    pallas_call x1, Pallas kernels: 52.1 us -> 50.4 us  [whole_heads(): pl.pallas_call(functools.partial(attention_kernel, seq, head), out_shape=...]
where the time goes in v4:
time: 55.2 us; the launch traced here: 54.3 us
  Pallas kernels  53 us (96%)
  between operations  1.3 us (2%)
    pallas_call x1, Pallas kernels, whole_heads(): pl.pallas_call(functools.partial(attention_kernel, seq, head), out_shape=...  50.4 us
    pallas_call x1, Pallas kernels, settle(): pl.pallas_call(functools.partial(settle_kernel, count), out_shape=[jax.Sh...  2.53 us

profile of v4, /device:TPU:0, one launch (start us, length us, event | category | flops | bytes accessed | tf_op | source)
XLA Modules:
  0.0 54.3 jit_solution(9588545117673610906)
XLA Ops:
  1.3 50.4 %whole_heads.1 = (bf16[32,1536]{1,0:T(8,128)(2,1)}, bf16[32,1536]{1,0:T(8,128)(2,1)}, bf16[32,1536]{1,0:T(8,128)(2,1)}, bf16[64,384]{1,0:T(8,128)(2,1)}, bf16[64...) custom-call(bf16[32,1536]{1,0:T(8,128)(2,1)} %q_in.1, ...), custom_call_target="tpu_custom_call" | custom-call | tf_op jit(solution)/shard_map/whole_heads/pallas_call | solution.py:918
  51.7 2.5 %settle.1 = (bf16[32,1536]{1,0:T(8,128)(2,1)}, bf16[32,1536]{1,0:T(8,128)(2,1)}, bf16[32,1536]{1,0:T(8,128)(2,1)}, bf16[64,384]{1,0:T(8,128)(2,1)}, bf16[64,384]...) custom-call(bf16[32,1536]{1,0:T(8,128)(2,1)} %get-tuple-element.27.refs, ...), custom_call_target="tpu_custom_call" | custom-call | tf_op jit(solution)/shard_map/settle/pallas_call | solution.py:875

commit v5 on v4

--- a/solution.py
+++ b/solution.py
@@ -578,7 +578,7 @@
         vall[image : 2 * image] = dequant(kv2[:, rows : 2 * rows])
         ktr[...] = kall[...].T
 
-        def query_block(index):
+        def weights(index):
             at = slice(index * half, (index + 1) * half)
             queries, grads = qall[at], doall[at]
             scores = dot(kall[...], queries, NT)
@@ -587,38 +587,38 @@
             expo = jnp.exp2(scores * (scale * math.log2(math.e)) - top)
             probs = expo * (1.0 / jnp.sum(expo, axis=0, keepdims=True))
             value_part = dot(probs.astype(BF), grads)
+            dvacc[...] = value_part if index == 0 else dvacc[...] + value_part
+            return probs, dprobs
+
+        def score_grads(probs, dprobs):
             deltas = jnp.sum(probs * dprobs, axis=0, keepdims=True)
-            dscores = (probs * (dprobs - deltas)).astype(BF)
-            key_part = dot(dscores, queries)
-            dvacc[...] = value_part if index == 0 else dvacc[...] + value_part
+            return (probs * (dprobs - deltas)).astype(BF)
+
+        def key_query(index, dscores):
+            at = slice(index * half, (index + 1) * half)
+            key_part = dot(dscores, qall[at])
             dkacc[...] = key_part if index == 0 else dkacc[...] + key_part
             dqall[at] = (dot(ktr[...], dscores).T * scale).astype(BF)
 
-        for index in range(image // half):
-            query_block(index)
+        last = image // half
+        for index in range(last):
+            key_query(index, score_grads(*weights(index)))
         for i in range(1, peers):
             back_query(lax.rem(me + i, peers)).start()
-        query_block(image // half)
+        last_weights = weights(last)
         xo[1] = dvacc[image : 2 * image].astype(BF)
         trade(1).start()
-        xo[0] = (dkacc[image : 2 * image] * scale).astype(BF)
-        trade(0).start()
+        last_grads = score_grads(*last_weights)
         trade(1).wait_recv()
         ost[:, 2 * rows : 3 * rows] = (
             (dvacc[0:image] + xi[1].astype(F32)).astype(BF).reshape(peers, rows, HEAD_SIZE)
         )
         for i in range(1, peers):
             back_send(2, lax.rem(me + i, peers)).start()
-        trade(0).wait_recv()
-        ost[:, rows : 2 * rows] = (
-            (dkacc[0:image] * scale + xi[0].astype(F32)).astype(BF).reshape(peers, rows, HEAD_SIZE)
-        )
-        for i in range(1, peers):
-            back_send(1, lax.rem(me + i, peers)).start()
-        ret[pl.ds(mine, 1), rows : 3 * rows] = ost[pl.ds(me, 1), rows : 3 * rows]
-        ret[pl.ds(mine, 1), 0:rows] = dqall[pl.ds(pl.multiple_of(me * rows, rows), rows)].reshape(
-            1, rows, HEAD_SIZE
-        )
+        ret[pl.ds(mine, 1), 2 * rows : 3 * rows] = ost[pl.ds(me, 1), 2 * rows : 3 * rows]
+        key_query(last, last_grads)
+        xo[0] = (dkacc[image : 2 * image] * scale).astype(BF)
+        trade(0).start()
 
         @pl.when(takes_text)
         def _():
@@ -672,6 +672,44 @@
     for i in range(1, seq):
         tile_send(lax.rem(s + i, seq)).start()
     low_in[pl.ds(s, 1)] = low_out[...].reshape(1, rows, HEAD_SIZE)
+
+    @pl.when(is_head)
+    def _():
+        trade(0).wait_recv()
+        ost[:, rows : 2 * rows] = (
+            (dkacc[0:image] * scale + xi[0].astype(F32)).astype(BF).reshape(peers, rows, HEAD_SIZE)
+        )
+        for i in range(1, peers):
+            back_send(1, lax.rem(me + i, peers)).start()
+        ret[pl.ds(mine, 1), rows : 2 * rows] = ost[pl.ds(me, 1), rows : 2 * rows]
+        ret[pl.ds(mine, 1), 0:rows] = dqall[pl.ds(pl.multiple_of(me * rows, rows), rows)].reshape(
+            1, rows, HEAD_SIZE
+        )
+
+    for i in range(1, seq):
+        t = lax.rem(s + i, seq)
+        send(xst.at[0], xcol.at[t], s6.at[0], r6.at[t], partner).wait_recv()
+        send(low_out, low_in.at[t], s10.at[0], r10.at[t], partner).wait_recv()
+
+    tiles = low_in[...]
+    flat = tiles.reshape(seq * rows, HEAD_SIZE).T
+    block = dot(flat, xcol[...].reshape(seq * rows, wide))[0:rank]
+    step_group = jnp.sum(tiles[:, 0:16].astype(F32), axis=0)
+    red_out[...] = block.astype(BF).reshape(head, part, wide)
+    sum_out[...] = step_group
+
+    def reduce_send(other):
+        return send(red_out.at[other], red_in.at[g], s11.at[0, other], r11.at[0, g], (s, other))
+
+    def sum_send(other):
+        return send(sum_out, sum_in.at[g], s11.at[1, other], r11.at[1, g], (s, other))
+
+    for i in range(1, head):
+        reduce_send(lax.rem(g + i, head)).start()
+    for i in range(1, head):
+        sum_send(lax.rem(g + i, head)).start()
+    red_in[pl.ds(g, 1)] = red_out[pl.ds(g, 1)]
+    sum_in[pl.ds(g, 1)] = step_group.reshape(1, 16, HEAD_SIZE)
 
     @pl.when(is_head)
     def _():
@@ -703,30 +741,6 @@
             up_send(lax.rem(me + i, peers)).start()
         up_all[pl.ds(mine, 1), pl.ds(c, 1)] = up_out[pl.ds(c, 1)].reshape(1, 1, hrank, HEAD_SIZE)
 
-    for i in range(1, seq):
-        t = lax.rem(s + i, seq)
-        send(xst.at[0], xcol.at[t], s6.at[0], r6.at[t], partner).wait_recv()
-        send(low_out, low_in.at[t], s10.at[0], r10.at[t], partner).wait_recv()
-
-    tiles = low_in[...]
-    flat = tiles.reshape(seq * rows, HEAD_SIZE).T
-    block = dot(flat, xcol[...].reshape(seq * rows, wide))[0:rank]
-    step_group = jnp.sum(tiles[:, 0:16].astype(F32), axis=0)
-    red_out[...] = block.astype(BF).reshape(head, part, wide)
-    sum_out[...] = step_group
-
-    def reduce_send(other):
-        return send(red_out.at[other], red_in.at[g], s11.at[0, other], r11.at[0, g], (s, other))
-
-    def sum_send(other):
-        return send(sum_out, sum_in.at[g], s11.at[1, other], r11.at[1, g], (s, other))
-
-    for i in range(1, head):
-        reduce_send(lax.rem(g + i, head)).start()
-    for i in range(1, head):
-        sum_send(lax.rem(g + i, head)).start()
-    red_in[pl.ds(g, 1)] = red_out[pl.ds(g, 1)]
-    sum_in[pl.ds(g, 1)] = step_group.reshape(1, 16, HEAD_SIZE)
     for i in range(1, head):
         other = lax.rem(g + i, head)
         send(red_out.at[0], red_in.at[other], s11.at[0, 0], r11.at[0, other], partner).wait_recv()

time: 55.2 us -> 57.9 us (1.049); the launches traced: 54.3 us -> 57.7 us
  Pallas kernels: 53 us -> 56.4 us
    pallas_call x1, Pallas kernels: 50.4 us -> 53.9 us  [whole_heads(): pl.pallas_call(functools.partial(attention_kernel, seq, head), out_shape=...]
where the time goes in v5:
time: 57.9 us; the launch traced here: 57.7 us
  Pallas kernels  56.4 us (97%)
  between operations  1.3 us (2%)
    pallas_call x1, Pallas kernels, whole_heads(): pl.pallas_call(functools.partial(attention_kernel, seq, head), out_shape=...  53.9 us
    pallas_call x1, Pallas kernels, settle(): pl.pallas_call(functools.partial(settle_kernel, count), out_shape=[jax.Sh...  2.53 us

profile of v5, /device:TPU:0, one launch (start us, length us, event | category | flops | bytes accessed | tf_op | source)
XLA Modules:
  0.0 57.7 jit_solution(5569568285349816254)
XLA Ops:
  1.3 53.9 %whole_heads.1 = (bf16[32,1536]{1,0:T(8,128)(2,1)}, bf16[32,1536]{1,0:T(8,128)(2,1)}, bf16[32,1536]{1,0:T(8,128)(2,1)}, bf16[64,384]{1,0:T(8,128)(2,1)}, bf16[64...) custom-call(bf16[32,1536]{1,0:T(8,128)(2,1)} %q_in.1, ...), custom_call_target="tpu_custom_call" | custom-call | tf_op jit(solution)/shard_map/whole_heads/pallas_call | solution.py:932
  55.2 2.5 %settle.1 = (bf16[32,1536]{1,0:T(8,128)(2,1)}, bf16[32,1536]{1,0:T(8,128)(2,1)}, bf16[32,1536]{1,0:T(8,128)(2,1)}, bf16[64,384]{1,0:T(8,128)(2,1)}, bf16[64,384]...) custom-call(bf16[32,1536]{1,0:T(8,128)(2,1)} %get-tuple-element.27.refs, ...), custom_call_target="tpu_custom_call" | custom-call | tf_op jit(solution)/shard_map/settle/pallas_call | solution.py:889

commit v6 on v4

--- a/solution.py
+++ b/solution.py
@@ -578,7 +578,7 @@
         vall[image : 2 * image] = dequant(kv2[:, rows : 2 * rows])
         ktr[...] = kall[...].T
 
-        def query_block(index):
+        def weights(index):
             at = slice(index * half, (index + 1) * half)
             queries, grads = qall[at], doall[at]
             scores = dot(kall[...], queries, NT)
@@ -587,38 +587,38 @@
             expo = jnp.exp2(scores * (scale * math.log2(math.e)) - top)
             probs = expo * (1.0 / jnp.sum(expo, axis=0, keepdims=True))
             value_part = dot(probs.astype(BF), grads)
+            dvacc[...] = value_part if index == 0 else dvacc[...] + value_part
+            return probs, dprobs
+
+        def score_grads(probs, dprobs):
             deltas = jnp.sum(probs * dprobs, axis=0, keepdims=True)
-            dscores = (probs * (dprobs - deltas)).astype(BF)
-            key_part = dot(dscores, queries)
-            dvacc[...] = value_part if index == 0 else dvacc[...] + value_part
+            return (probs * (dprobs - deltas)).astype(BF)
+
+        def key_query(index, dscores):
+            at = slice(index * half, (index + 1) * half)
+            key_part = dot(dscores, qall[at])
             dkacc[...] = key_part if index == 0 else dkacc[...] + key_part
             dqall[at] = (dot(ktr[...], dscores).T * scale).astype(BF)
 
-        for index in range(image // half):
-            query_block(index)
+        last = image // half
+        for index in range(last):
+            key_query(index, score_grads(*weights(index)))
         for i in range(1, peers):
             back_query(lax.rem(me + i, peers)).start()
-        query_block(image // half)
+        last_weights = weights(last)
         xo[1] = dvacc[image : 2 * image].astype(BF)
         trade(1).start()
-        xo[0] = (dkacc[image : 2 * image] * scale).astype(BF)
-        trade(0).start()
+        last_grads = score_grads(*last_weights)
         trade(1).wait_recv()
         ost[:, 2 * rows : 3 * rows] = (
             (dvacc[0:image] + xi[1].astype(F32)).astype(BF).reshape(peers, rows, HEAD_SIZE)
         )
         for i in range(1, peers):
             back_send(2, lax.rem(me + i, peers)).start()
-        trade(0).wait_recv()
-        ost[:, rows : 2 * rows] = (
-            (dkacc[0:image] * scale + xi[0].astype(F32)).astype(BF).reshape(peers, rows, HEAD_SIZE)
-        )
-        for i in range(1, peers):
-            back_send(1, lax.rem(me + i, peers)).start()
-        ret[pl.ds(mine, 1), rows : 3 * rows] = ost[pl.ds(me, 1), rows : 3 * rows]
-        ret[pl.ds(mine, 1), 0:rows] = dqall[pl.ds(pl.multiple_of(me * rows, rows), rows)].reshape(
-            1, rows, HEAD_SIZE
-        )
+        ret[pl.ds(mine, 1), 2 * rows : 3 * rows] = ost[pl.ds(me, 1), 2 * rows : 3 * rows]
+        key_query(last, last_grads)
+        xo[0] = (dkacc[image : 2 * image] * scale).astype(BF)
+        trade(0).start()
 
         @pl.when(takes_text)
         def _():
@@ -626,6 +626,17 @@
             to[text : 2 * text] = dvacc[2 * image : 2 * image + text].astype(BF)
             to[2 * text : 2 * text + half] = dqall[image : image + half]
             text_trade().start()
+
+        trade(0).wait_recv()
+        ost[:, rows : 2 * rows] = (
+            (dkacc[0:image] * scale + xi[0].astype(F32)).astype(BF).reshape(peers, rows, HEAD_SIZE)
+        )
+        for i in range(1, peers):
+            back_send(1, lax.rem(me + i, peers)).start()
+        ret[pl.ds(mine, 1), rows : 2 * rows] = ost[pl.ds(me, 1), rows : 2 * rows]
+        ret[pl.ds(mine, 1), 0:rows] = dqall[pl.ds(pl.multiple_of(me * rows, rows), rows)].reshape(
+            1, rows, HEAD_SIZE
+        )
 
         for i in range(1, peers):
             p = lax.rem(me + i, peers)
@@ -727,6 +738,7 @@
         sum_send(lax.rem(g + i, head)).start()
     red_in[pl.ds(g, 1)] = red_out[pl.ds(g, 1)]
     sum_in[pl.ds(g, 1)] = step_group.reshape(1, 16, HEAD_SIZE)
+
     for i in range(1, head):
         other = lax.rem(g + i, head)
         send(red_out.at[0], red_in.at[other], s11.at[0, 0], r11.at[0, other], partner).wait_recv()

time: 55.2 us -> 55 us (level)
  no operation moved by 1% of the time
where the time goes in v6:
time: 55 us; the launch traced here: 54.1 us
  Pallas kernels  52.8 us (96%)
  between operations  1.3 us (2%)
    pallas_call x1, Pallas kernels, whole_heads(): pl.pallas_call(functools.partial(attention_kernel, seq, head), out_shape=...  50.3 us
    pallas_call x1, Pallas kernels, settle(): pl.pallas_call(functools.partial(settle_kernel, count), out_shape=[jax.Sh...  2.53 us

profile of v6, /device:TPU:0, one launch (start us, length us, event | category | flops | bytes accessed | tf_op | source)
XLA Modules:
  0.0 54.1 jit_solution(9583738989693660525)
XLA Ops:
  1.3 50.3 %whole_heads.1 = (bf16[32,1536]{1,0:T(8,128)(2,1)}, bf16[32,1536]{1,0:T(8,128)(2,1)}, bf16[32,1536]{1,0:T(8,128)(2,1)}, bf16[64,384]{1,0:T(8,128)(2,1)}, bf16[64...) custom-call(bf16[32,1536]{1,0:T(8,128)(2,1)} %q_in.1, ...), custom_call_target="tpu_custom_call" | custom-call | tf_op jit(solution)/shard_map/whole_heads/pallas_call | solution.py:930
  51.6 2.5 %settle.1 = (bf16[32,1536]{1,0:T(8,128)(2,1)}, bf16[32,1536]{1,0:T(8,128)(2,1)}, bf16[32,1536]{1,0:T(8,128)(2,1)}, bf16[64,384]{1,0:T(8,128)(2,1)}, bf16[64,384]...) custom-call(bf16[32,1536]{1,0:T(8,128)(2,1)} %get-tuple-element.27.refs, ...), custom_call_target="tpu_custom_call" | custom-call | tf_op jit(solution)/shard_map/settle/pallas_call | solution.py:887
